TPU v7x, 32 devices: a whole 2x2x4 slice. The times are simulated.
32 devices in a mesh: row: 4 (over y, x), col: 8 (over z, core).
Axes of the slice: x: 2, y: 2, z: 4, core: 2. Of those that a mesh axis runs over, the one named last changes fastest.
Arguments:
- features: bfloat16 [4096, 256], P(('row', 'col')), may hold values from -6 to 6
- weight: bfloat16 [256, 256], replicated, may hold values from -0.375 to 0.375
- tiles: bfloat16 [384, 128, 128], P(('row', 'col')), may hold values from 0 to 0.0099487305
- tile_pos: int32 [384], P(('row', 'col')), may hold values from -1 to 31, as said below
- edge_keep: int32 [2, 384], P(None, ('row', 'col')), may hold values 0 or 1
- feature_keep: int32 [2, 256], replicated, may hold values 0 or 1
- negatives: int32 [4096, 1024], P(('row', 'col')), may hold values from 0 to 511, as said below
Outputs:
- node_loss: float32 [4096], P(('row', 'col'))
- weight_grad: float32 [256, 256], replicated
Inputs may be any that keep to these rules, and one draw needn't show every extreme that they name: `tile_pos`: on each device the first count slots hold distinct positions and the rest are -1; every device has at least one tile, at least one device has all 12 slots filled. `negatives`: indices into the node's column group, each node's list in ascending order; an index may repeat within a node's list.
All inputs are finite; a program needn't handle non-finite values. No bound on the sum of `edge_keep` on one device may be relied on, other than what follows from the above.
Results may differ from a plain program's by a relative error of at most 0.0035.
Values may be sent and summed in bfloat16 or wider, within the bound.
A program may use at most 64 MiB of HBM per device.

v0:
```python
import jax
import jax.numpy as jnp
from jax import lax
from jax.sharding import PartitionSpec as P

tau = 0.5
eps = 1e-06


def shards(features, weight, tiles, tile_pos, edge_keep, feature_keep, negatives):
    nodes_here, width = features.shape
    row_count = lax.axis_size("row")
    col_count = lax.axis_size("col")
    tile_rows = row_count * nodes_here // 128
    tile_cols = col_count * nodes_here // 128
    group = row_count * nodes_here
    rowgroup = lax.all_gather(features, "col", axis=0, tiled=True)
    xrows = rowgroup.reshape(tile_cols, 128, width)
    valid = (tile_pos >= 0).astype(jnp.float32)
    clamped = jnp.maximum(tile_pos, 0)
    trow = clamped // tile_cols
    tcol = clamped % tile_cols
    weights_kept = edge_keep.astype(jnp.float32) * valid[None, :]
    product = jnp.einsum("kab,kbf->kaf", tiles, xrows[tcol], preferred_element_type=jnp.float32)
    onehot = (trow[None, :] == jnp.arange(tile_rows)[:, None]).astype(jnp.float32)
    mixing = weights_kept[:, None, :] * onehot[None, :, :]
    summed = jnp.einsum("vtk,kaf->vtaf", mixing, product, precision=lax.Precision.HIGHEST)
    partial_value = summed.reshape(2, group, width).astype(jnp.bfloat16)
    agg = lax.psum_scatter(partial_value, "row", scatter_dimension=1, tiled=True).astype(
        jnp.float32
    )
    agg = agg * feature_keep.astype(jnp.float32)[:, None, :]
    agg_b = agg.astype(jnp.bfloat16)
    z_vals = jnp.einsum("vnf,fg->vng", agg_b, weight, preferred_element_type=jnp.float32)
    rinv = lax.rsqrt(jnp.sum(z_vals * z_vals, -1, keepdims=True) + eps)
    emb = z_vals * rinv
    emb_b = emb.astype(jnp.bfloat16)
    grouped = lax.all_gather(emb_b, "row", axis=1, tiled=True)
    hb1, hb2 = (emb_b[0], emb_b[1])
    h1f, h2f = (hb1.astype(jnp.float32), hb2.astype(jnp.float32))
    counts = (
        jnp.zeros((nodes_here, group), jnp.float32)
        .at[jnp.arange(nodes_here)[:, None], negatives]
        .add(1.0)
    )
    pos = jnp.sum(h1f * h2f, -1) / tau
    s12 = jnp.dot(hb1, grouped[1].T, preferred_element_type=jnp.float32) / tau
    s21 = jnp.dot(hb2, grouped[0].T, preferred_element_type=jnp.float32) / tau
    e12 = counts * jnp.exp(s12)
    e21 = counts * jnp.exp(s21)
    tot1 = jnp.exp(pos) + jnp.sum(e12, 1)
    tot2 = jnp.exp(pos) + jnp.sum(e21, 1)
    node_loss = 0.5 * (jnp.log(tot1) - pos + (jnp.log(tot2) - pos))
    coef = 1.0 / (2.0 * tau * jnp.sqrt(jnp.float32(row_count * col_count * nodes_here)))
    p_one = jnp.exp(pos) / tot1
    p_two = jnp.exp(pos) / tot2
    q_one = (e12 / tot1[:, None]).astype(jnp.bfloat16)
    q_two = (e21 / tot2[:, None]).astype(jnp.bfloat16)
    recv_one, recv_two = (
        lax.all_to_all(q_one, "row", split_axis=1, concat_axis=0, tiled=True),
        lax.all_to_all(q_two, "row", split_axis=1, concat_axis=0, tiled=True),
    )
    back_one = coef * jnp.dot(recv_two.T, grouped[1], preferred_element_type=jnp.float32)
    back_two = coef * jnp.dot(recv_one.T, grouped[0], preferred_element_type=jnp.float32)
    both = (p_one + p_two - 2.0)[:, None]
    d_one = (
        coef * (both * h2f + jnp.dot(q_one, grouped[1], preferred_element_type=jnp.float32))
        + back_one
    )
    d_two = (
        coef * (both * h1f + jnp.dot(q_two, grouped[0], preferred_element_type=jnp.float32))
        + back_two
    )
    d_both = jnp.stack([d_one, d_two])
    dz_vals = (d_both - emb * jnp.sum(emb * d_both, -1, keepdims=True)) * rinv
    local_grad = jnp.einsum(
        "vnf,vng->fg", agg_b.astype(jnp.float32), dz_vals, precision=lax.Precision.HIGHEST
    )
    weight_grad = lax.psum(local_grad, ("row", "col"))
    return (node_loss, weight_grad)


def solution(mesh):
    in_specs = (
        P(("row", "col"), None),
        P(),
        P(("row", "col"), None, None),
        P(("row", "col")),
        P(None, ("row", "col")),
        P(),
        P(("row", "col"), None),
    )
    out_specs = (P(("row", "col")), P())
    return jax.shard_map(shards, mesh=mesh, in_specs=in_specs, out_specs=out_specs, check_vma=False)
```

profile of v0, /device:TPU:0, one launch (start us, length us, event | category | flops | bytes accessed | tf_op | source)
XLA Modules:
  0.0 1105.6 jit_solution(13956097408004592841)
XLA Ops:
  7.2 0.7 and_select_fusion.1
  7.9 0.7 compare_convert_fusion
  8.6 16.8 %all_gather.6 = bf16[1024,256]{1,0:T(8,128)(2,1)S(1)} all-gather(bf16[128,256]{1,0:T(8,128)(2,1)} %param.7), channel_id=1, replica_groups=mesh['row'=4,'col'=8] {'col'}, dimensions={0}, use_global_device_ids=true | all-gather | bytes 589824 | tf_op jit(solution)/shard_map/all_gather | solution.py:17
  25.4 0.6 gather_fusion
  26.0 1.6 fusion.35
  27.6 2.2 copy.14
  29.9 1.7 fusion.2
  31.5 0.9 copy.10
  32.7 0.3 copy-done.7
  33.5 903.7 %scatter_custom_fusion = f32[65536]{0:T(1024)S(1)} fusion(s32[131072]{0:T(1024)S(1)} %bitcast.88, f32[131072]{0:T(1024)S(1)} %broadcast.92, f32[]{:T(128)} %constant.50.clone.1), kind=kCustom, calls=%fused_computation.47 | custom fusion | flops 131072 | bytes 262148
  937.3 1.2 multiply_reduce_fusion.2
  938.6 10.4 all_gather.7
  949.0 0.3 fusion.34
  949.3 0.3 fusion.33
  949.7 0.5 add_add_fusion
  950.3 0.7 copy_bitcast_fusion.1
  951.0 3.3 all-to-all-start
  954.8 0.8 copy_bitcast_fusion
  955.6 3.7 all-to-all-done
  959.3 3.3 all-to-all-start.1
  962.9 4.7 all-to-all-done.1
  968.1 1.1 convolution_bitcast_fusion
  969.2 127.9 %all-reduce.2.cloned.1.call-done = f32[256,256]{1,0:T(8,128)} async-done(((f32[256,256]{1,0:T(8,128)}), f32[256,256]{1,0:T(8,128)}) %all-reduce.2.cloned.1.call-update) | async-done | bytes 262160 | tf_op jit(solution)/shard_map/psum | solution.py:79
  1097.1 1.7 copy.23
  (40 shorter events, 2.3 us)
Async XLA Ops:
  7.2 18.8 %copy-start = (bf16[12,128,128]{2,1,0:T(8,128)(2,1)S(1)}, bf16[12,128,128]{2,1,0:T(8,128)(2,1)}, u32[]{:S(2)}) copy-start(bf16[12,128,128]{2,1,0:T(8,128)(2,1)} %param.9) | copy-start | bytes 1179652
  7.2 930.1 %reduce-scatter.2.cloned.1.call-start = ((), (), s32[]{:S(2)}) async-start(), calls=%async_computation.3 | async-start | bytes 655360 | tf_op jit(solution)/shard_map/reduce_scatter | solution.py:29
  27.6 2.3 copy-start.5
  29.8 2.6 copy-start.4
  29.8 2.6 copy-start.1
  31.5 1.0 copy-start.6
  32.4 0.7 copy-start.7
  33.0 904.2 %copy-start.3 = (bf16[256,256]{1,0:T(8,128)(2,1)S(1)}, bf16[256,256]{1,0:T(8,128)(2,1)}, u32[]{:S(2)}) copy-start(bf16[256,256]{1,0:T(8,128)(2,1)} %param.8) | copy-start | bytes 393220
  951.0 8.3 all-to-all-start
  954.6 13.5 %copy-start.2 = (bf16[2,128,256]{2,1,0:T(8,128)(2,1)S(1)}, bf16[2,128,256]{2,1,0:T(8,128)(2,1)}, u32[]{:S(2)}) copy-start(bf16[2,128,256]{2,1,0:T(8,128)(2,1)} %reduce-scatter.2.cloned.1.call-done) | copy-start | bytes 393220
  959.3 8.3 all-to-all-start.1
  962.7 134.4 %all-reduce.2.cloned.1.call-start = ((), (), s32[]{:S(2)}) async-start(), calls=%async_computation.4 | async-start | bytes 524288 | tf_op jit(solution)/shard_map/psum | solution.py:79
Sparse Core Ops, SparseCore 0:
  32.5 25.8 reduce-scatter.1
  970.5 126.5 all-reduce.1
where the time goes:
time: 1110 us
  other arithmetic  908 us (82%)
  waiting for transfers between devices  136 us (12%)
  blocking collectives  27.2 us (2%)
  between operations  14.3 us (1%)
    unnamed x4, other arithmetic  904 us
    psum x1, waiting for transfers between devices, shards(): weight_grad = lax.psum(local_grad, ('row', 'col'))  128 us
  transfers between devices with their start and end apart: 4, of which 3 were waited for; matrix products, arithmetic and copies ran while one was open for 82% of the time, Pallas kernels for 0%

commit v1 on v0

v1 whole, which is shorter than its diff:
```python
import functools

import jax
import jax.numpy as jnp
from jax import lax
from jax.experimental import pallas as pl
from jax.experimental.pallas import tpu as pltpu
from jax.sharding import PartitionSpec as P

tau = 0.5
eps = 1e-06
F32 = jnp.float32
BF16 = jnp.bfloat16
MESH = pl.DeviceIdType.MESH


def loop(start, stop, body):
    if stop - start <= 8:
        for i in range(start, stop):
            body(i)
    else:
        def step(i, carry):
            body(i)
            return carry
        lax.fori_loop(start, stop, step, 0)


def count_kernel(neg_ref, cnt_ref):
    rows, n_neg = neg_ref.shape
    blocks = cnt_ref.shape[1] // 128
    chunks = n_neg // 128
    per = 4 if blocks % 4 == 0 else 1
    lane = lax.broadcasted_iota(jnp.int32, (8, 128), 1)

    def rank(parts, target):
        total = jnp.zeros((8, 128), jnp.int32)
        for part in parts:
            low = jnp.zeros((8, 128), jnp.int32)
            for step in (64, 32, 16, 8, 4, 2, 1):
                seen = jnp.take_along_axis(part, low + (step - 1), axis=1, mode="promise_in_bounds")
                low = jnp.where(seen <= target, low + step, low)
            seen = jnp.take_along_axis(part, low, axis=1, mode="promise_in_bounds")
            total = total + jnp.where(seen <= target, low + 1, low)
        return total

    def row_step(i, carry):
        base = pl.multiple_of(i * 8, 8)
        parts = [neg_ref[pl.ds(base, 8), k * 128 : (k + 1) * 128] for k in range(chunks)]

        def block_step(g, before):
            for j in range(per):
                at = pl.multiple_of((g * per + j) * 128, 128)
                now = rank(parts, lane + at)
                rolled = pltpu.roll(now, 1, 1)
                shifted = jnp.where(lane == 0, before, rolled)
                cnt_ref[pl.ds(base, 8), pl.ds(at, 128)] = (now - shifted).astype(F32)
                before = rolled
            return before

        first = jnp.zeros((8, 128), jnp.int32)
        if blocks == per:
            block_step(0, first)
        else:
            lax.fori_loop(0, blocks // per, block_step, first)
        return carry

    lax.fori_loop(0, rows // 8, row_step, 0)


def step_kernel(
    R, C,
    feat, weight, tiles, pos_ref, keep_ref, fkeep, cnt,
    loss_out, grad_out,
    xg, xcat, pbuf, rbuf, gbuf, embf, embb, rinv, eb, wacc, wbuf, wr, ws, wc, wd, obuf,
    f_send, f_recv, s_send, s_recv, p_send, p_recv, g_send, g_recv,
    a_send, a_recv, b_send, b_recv, c_send, c_recv, d_send, d_recv,
):
    nodes, width = feat.shape
    slots = tiles.shape[0]
    chips = C // 2
    cr = wr.shape[1]
    cc = wc.shape[1]
    me_r = lax.axis_index("row")
    me_c = lax.axis_index("col")
    chip = me_c // 2
    core = me_c % 2
    sib = chip * 2 + (1 - core)

    def at_row(o):
        return lax.rem(me_r + o, R)

    def from_row(o):
        return lax.rem(me_r + R - o, R)

    def at_col(o):
        return lax.rem(me_c + o, C)

    def from_col(o):
        return lax.rem(me_c + C - o, C)

    def copy(src, dst, send, recv, r, c):
        return pltpu.make_async_remote_copy(
            src_ref=src, dst_ref=dst, send_sem=send, recv_sem=recv,
            device_id=(r, c), device_id_type=MESH,
        )

    barrier = pltpu.get_barrier_semaphore()
    loop(1, R, lambda o: pl.semaphore_signal(barrier, inc=1, device_id=(at_row(o), me_c), device_id_type=MESH))
    loop(1, C, lambda o: pl.semaphore_signal(barrier, inc=1, device_id=(me_r, at_col(o)), device_id_type=MESH))
    pl.semaphore_wait(barrier, R + C - 2)

    def far(o):
        to = lax.rem(chip + o, chips) * 2 + core
        return copy(feat, xg.at[me_c], f_send.at[o], f_recv.at[o], me_r, to)

    def near(o):
        if isinstance(o, int) and o == 0:
            return copy(feat, xg.at[me_c], s_send.at[0], s_recv.at[0], me_r, sib)
        slot = lax.rem(chip + chips - o, chips) * 2 + core
        return copy(xg.at[slot], xg.at[slot], s_send.at[o], s_recv.at[o], me_r, sib)

    loop(1, chips, lambda o: far(o).start())
    near(0).start()
    xg[me_c] = feat[...]

    def pass_on(o):
        far(o).wait_recv()
        near(o).start()

    loop(1, chips, pass_on)
    near(0).wait_recv()
    loop(1, chips, lambda o: near(o).wait_recv())

    where = [jnp.maximum(pos_ref[k], 0) for k in range(slots)]
    trow = [w // C for w in where]
    live = [[keep_ref[v, k] * (pos_ref[k] >= 0).astype(jnp.int32) for k in range(slots)] for v in range(2)]
    for k in range(slots):
        xcat[k * 128 : (k + 1) * 128, :] = xg[lax.rem(where[k], C)]

    def part_copy(o):
        return copy(pbuf.at[o], rbuf.at[o], p_send.at[o], p_recv.at[o], at_row(o), me_c)

    def part(o):
        t = at_row(o)
        out = []
        for v in range(2):
            lhs = []
            for k in range(slots):
                use = jnp.where(trow[k] == t, live[v][k], 0).astype(F32)
                lhs.append(tiles[k] * jnp.full((1, 128), use, F32).astype(BF16))
            out.append(jnp.dot(jnp.concatenate(lhs, axis=1), xcat[...], preferred_element_type=F32).astype(BF16))
        return out

    def part_send(o):
        first, second = part(o)
        pbuf[o, 0] = first
        pbuf[o, 1] = second
        part_copy(o).start()

    loop(1, R, part_send)
    mine = part(0)
    pbuf[0, 0] = mine[0]
    pbuf[0, 1] = mine[1]
    loop(1, R, lambda o: part_copy(o).wait_recv())

    for v in range(2):
        total = pbuf[0, v].astype(F32)
        if R <= 8:
            for o in range(1, R):
                total = total + rbuf[o, v].astype(F32)
        else:
            total = lax.fori_loop(1, R, lambda o, acc: acc + rbuf[o, v].astype(F32), total)
        total = total * fkeep[v : v + 1, :].astype(F32)
        gbuf[me_r, v] = total.astype(BF16)

    def agg_copy(o):
        return copy(gbuf.at[me_r], gbuf.at[me_r], g_send.at[o], g_recv.at[o], at_row(o), me_c)

    loop(1, R, lambda o: agg_copy(o).start())

    def embed(r):
        for v in range(2):
            z = jnp.dot(gbuf[r, v], weight[...], preferred_element_type=F32)
            scale = lax.rsqrt(jnp.sum(z * z, -1, keepdims=True) + eps)
            emb = z * scale
            rinv[r, v] = scale
            embf[r, v] = emb
            embb[r, v] = emb.astype(BF16)

    embed(me_r)
    h1 = embb[me_r, 0]
    h2 = embb[me_r, 1]
    h1f = h1.astype(F32)
    h2f = h2.astype(F32)
    pos = jnp.sum(h1f * h2f, -1, keepdims=True) / tau
    NT = (((1,), (1,)), ((), ()))
    TN = (((0,), (0,)), ((), ()))

    def scores(r):
        cols = pl.ds(pl.multiple_of(r * 128, 128), 128)
        counts = cnt[:, cols]
        s12 = lax.dot_general(h1, embb[r, 1], NT, preferred_element_type=F32) / tau
        s21 = lax.dot_general(h2, embb[r, 0], NT, preferred_element_type=F32) / tau
        eb[r, 0] = counts * jnp.exp(s12)
        eb[r, 1] = counts * jnp.exp(s21)

    scores(me_r)

    def arrived(o):
        r = from_row(o)
        agg_copy(o).wait_recv()
        embed(r)
        scores(r)

    loop(1, R, arrived)

    def row_sum(v):
        if R <= 8:
            total = eb[0, v]
            for r in range(1, R):
                total = total + eb[r, v]
        else:
            total = lax.fori_loop(1, R, lambda r, acc: acc + eb[r, v], eb[0, v])
        return jnp.sum(total, 1, keepdims=True)

    epos = jnp.exp(pos)
    tot1 = epos + row_sum(0)
    tot2 = epos + row_sum(1)
    loss = 0.5 * (jnp.log(tot1) - pos + (jnp.log(tot2) - pos))
    loss_out[...] = jnp.broadcast_to(loss, (nodes, 128)).T[0:1, :]
    both = epos / tot1 + epos / tot2 - 2.0
    coef = 1.0 / (2.0 * tau * float(R * C * nodes) ** 0.5)

    def dz_term(r, d_one, d_two):
        parts = []
        for v, d in enumerate((d_one, d_two)):
            emb = embf[r, v]
            dz = (d - emb * jnp.sum(emb * d, -1, keepdims=True)) * rinv[r, v]
            high = dz.astype(BF16)
            low = (dz - high.astype(F32)).astype(BF16)
            parts.append(jnp.concatenate([high, low], axis=1))
        rhs = jnp.concatenate(parts, axis=0)
        lhs = jnp.concatenate([gbuf[r, 0], gbuf[r, 1]], axis=0)
        return lax.dot_general(lhs, rhs, TN, preferred_element_type=F32)

    def weights(r):
        q1 = (eb[r, 0] / tot1).astype(BF16)
        q2 = (eb[r, 1] / tot2).astype(BF16)
        fore1 = jnp.dot(q1, embb[r, 1], preferred_element_type=F32)
        fore2 = jnp.dot(q2, embb[r, 0], preferred_element_type=F32)
        back1 = lax.dot_general(q2, h2, TN, preferred_element_type=F32)
        back2 = lax.dot_general(q1, h1, TN, preferred_element_type=F32)
        return fore1, fore2, back1, back2

    acc1, acc2, own1, own2 = weights(me_r)
    wacc[...] = jnp.zeros_like(wacc)

    def other(o, carry):
        r = from_row(o)
        fore1, fore2, back1, back2 = weights(r)
        wacc[...] += dz_term(r, coef * back1, coef * back2)
        return carry[0] + fore1, carry[1] + fore2

    if R <= 8:
        for o in range(1, R):
            acc1, acc2 = other(o, (acc1, acc2))
    else:
        acc1, acc2 = lax.fori_loop(1, R, other, (acc1, acc2))
    both_terms = wacc[...] + dz_term(
        me_r, coef * (both * h2f + acc1 + own1), coef * (both * h1f + acc2 + own2)
    )
    if wbuf.shape[0] > width:
        wbuf[...] = jnp.zeros_like(wbuf)
    wbuf[0:width, :] = both_terms[:, :width] + both_terms[:, width:]

    def a_copy(o):
        rows = pl.ds(pl.multiple_of(at_row(o) * cr, 8), cr)
        return copy(wbuf.at[rows, :], wr.at[o], a_send.at[o], a_recv.at[o], at_row(o), me_c)

    loop(1, R, lambda o: a_copy(o).start())
    own = wbuf[pl.ds(pl.multiple_of(me_r * cr, 8), cr), :]
    if ws.shape[0] > cr:
        ws[...] = jnp.zeros_like(ws)
    loop(1, R, lambda o: a_copy(o).wait_recv())
    if R <= 8:
        for o in range(1, R):
            own = own + wr[o]
    else:
        own = lax.fori_loop(1, R, lambda o, acc: acc + wr[o], own)
    ws[0:cr, :] = own

    def b_copy(o):
        rows = pl.ds(pl.multiple_of(at_col(o) * cc, 8), cc)
        return copy(ws.at[rows, :], wc.at[o], b_send.at[o], b_recv.at[o], me_r, at_col(o))

    loop(1, C, lambda o: b_copy(o).start())
    piece = ws[pl.ds(pl.multiple_of(me_c * cc, 8), cc), :]
    loop(1, C, lambda o: b_copy(o).wait_recv())
    if C <= 8:
        for o in range(1, C):
            piece = piece + wc[o]
    else:
        piece = lax.fori_loop(1, C, lambda o, acc: acc + wc[o], piece)
    mine_rows = pl.ds(pl.multiple_of(me_c * cc, 8), cc)
    wd[mine_rows, :] = piece

    def c_copy(o):
        return copy(wd.at[mine_rows, :], wd.at[mine_rows, :], c_send.at[o], c_recv.at[o], me_r, at_col(o))

    loop(1, C, lambda o: c_copy(o).start())
    loop(1, C, lambda o: c_copy(o).wait_recv())
    my_out = pl.ds(pl.multiple_of(me_r * cr, 8), cr)

    def d_copy(o):
        return copy(wd.at[pl.ds(0, cr), :], obuf.at[my_out, :], d_send.at[o], d_recv.at[o], at_row(o), me_c)

    loop(1, R, lambda o: d_copy(o).start())
    obuf[my_out, :] = wd[0:cr, :]
    loop(1, R, lambda o: d_copy(o).wait_recv())
    grad_out[...] = obuf[0:width, :]

    loop(1, chips, lambda o: far(o).wait_send())
    near(0).wait_send()
    loop(1, chips, lambda o: near(o).wait_send())
    loop(1, R, lambda o: part_copy(o).wait_send())
    loop(1, R, lambda o: agg_copy(o).wait_send())
    loop(1, R, lambda o: a_copy(o).wait_send())
    loop(1, C, lambda o: b_copy(o).wait_send())
    loop(1, C, lambda o: c_copy(o).wait_send())
    loop(1, R, lambda o: d_copy(o).wait_send())


def up(n, d, unit):
    return -(-(-(-n // d)) // unit) * unit


def shards(features, weight, tiles, tile_pos, edge_keep, feature_keep, negatives):
    nodes, width = features.shape
    slots = tiles.shape[0]
    R = lax.axis_size("row")
    C = lax.axis_size("col")
    group = R * nodes
    chips = C // 2
    counts = pl.pallas_call(
        count_kernel,
        out_shape=jax.ShapeDtypeStruct((nodes, group), F32),
        in_specs=[pl.BlockSpec(memory_space=pltpu.VMEM)],
        out_specs=pl.BlockSpec(memory_space=pltpu.VMEM),
        compiler_params=pltpu.CompilerParams(vmem_limit_bytes=16 << 20),
    )(negatives)
    cr = up(width, R, 8)
    cc = up(cr, C, 8)
    vmem = pl.BlockSpec(memory_space=pltpu.VMEM)
    smem = pl.BlockSpec(memory_space=pltpu.SMEM)
    sem = pltpu.SemaphoreType.DMA
    loss, grad = pl.pallas_call(
        functools.partial(step_kernel, R, C),
        out_shape=(
            jax.ShapeDtypeStruct((1, nodes), F32),
            jax.ShapeDtypeStruct((width, width), F32),
        ),
        in_specs=[vmem, vmem, vmem, smem, smem, vmem, vmem],
        out_specs=(vmem, vmem),
        scratch_shapes=[
            pltpu.VMEM((C, nodes, width), BF16),
            pltpu.VMEM((slots * 128, width), BF16),
            pltpu.VMEM((R, 2, nodes, width), BF16),
            pltpu.VMEM((R, 2, nodes, width), BF16),
            pltpu.VMEM((R, 2, nodes, width), BF16),
            pltpu.VMEM((R, 2, nodes, width), F32),
            pltpu.VMEM((R, 2, nodes, width), BF16),
            pltpu.VMEM((R, 2, nodes, 1), F32),
            pltpu.VMEM((R, 2, nodes, 128), F32),
            pltpu.VMEM((width, 2 * width), F32),
            pltpu.VMEM((R * cr, width), F32),
            pltpu.VMEM((R, cr, width), F32),
            pltpu.VMEM((C * cc, width), F32),
            pltpu.VMEM((C, cc, width), F32),
            pltpu.VMEM((C * cc, width), F32),
            pltpu.VMEM((R * cr, width), F32),
            sem((chips,)), sem((chips,)), sem((chips,)), sem((chips,)),
            sem((R,)), sem((R,)), sem((R,)), sem((R,)),
            sem((R,)), sem((R,)), sem((C,)), sem((C,)),
            sem((C,)), sem((C,)), sem((R,)), sem((R,)),
        ],
        compiler_params=pltpu.CompilerParams(
            collective_id=0, has_side_effects=True, vmem_limit_bytes=48 << 20
        ),
    )(features, weight, tiles, tile_pos, edge_keep, feature_keep, counts)
    return loss.reshape(nodes), grad


def solution(mesh):
    in_specs = (
        P(("row", "col"), None),
        P(),
        P(("row", "col"), None, None),
        P(("row", "col")),
        P(None, ("row", "col")),
        P(),
        P(("row", "col"), None),
    )
    out_specs = (P(("row", "col")), P())
    return jax.shard_map(shards, mesh=mesh, in_specs=in_specs, out_specs=out_specs, check_vma=False)
```

time: 1110 us -> 66.6 us (0.06)
  other arithmetic: 908 us -> 0 us
  waiting for transfers between devices: 136 us -> 0 us
  Pallas kernels: 0 us -> 63.5 us
  blocking collectives: 27.2 us -> 0 us
  between operations: 14.3 us -> 0.71 us
    unnamed x4 -> x0, other arithmetic: 904 us -> none
    psum x1 -> x0, waiting for transfers between devices: 128 us -> none  [shards(): weight_grad = lax.psum(local_grad, ('row', 'col'))]
    pallas_call x0 -> x2, Pallas kernels: none -> 63.5 us  [the longest x1 50 us: shards(): pl.pallas_call(functools.partial(step_kernel, R, C), out_shape=(jax.Shape...]
    all_gather x2 -> x0, blocking collectives: 27.2 us -> none  [the longest x1 16.8 us: shards(): rowgroup = lax.all_gather(features, 'col', axis=0, tiled=True)]
  transfers between devices with their start and end apart: 4 -> 0, of which waited for: 3 -> 0; matrix products, arithmetic and copies ran while one was open for 82% -> 0% of each run, Pallas kernels for 0% -> 0%
where the time goes in v1:
time: 66.6 us; the launch traced here: 66.4 us
  Pallas kernels  63.5 us (95%)
  local copies, waits for them, and re-layouts  2.27 us (3%)
  between operations  0.71 us (1%)
    pallas_call x1, Pallas kernels, shards(): pl.pallas_call(functools.partial(step_kernel, R, C), out_shape=(jax.Shape...  50 us
    pallas_call x1, Pallas kernels, shards(): pl.pallas_call(count_kernel, out_shape=jax.ShapeDtypeStruct((nodes, group...  13.5 us
    unnamed x16, local copies, waits for them, and re-layouts  2.27 us

profile of v1, /device:TPU:0, one launch (start us, length us, event | category | flops | bytes accessed | tf_op | source)
XLA Modules:
  0.0 66.4 jit_solution(5157174603049865719)
XLA Ops:
  0.6 0.0 copy-start
  0.6 1.0 %copy-done = s32[128,1024]{1,0:T(8,128)S(1)} copy-done((s32[128,1024]{1,0:T(8,128)S(1)}, s32[128,1024]{1,0:T(8,128)}, u32[]{:S(2)}) %copy-start) | copy-done | bytes 524312
  1.7 0.0 copy-start.1
  1.7 0.0 copy-start.2
  1.7 0.0 copy-start.3
  1.7 0.0 copy-start.4
  1.7 0.0 copy-start.5
  1.7 0.0 copy-start.6
  1.7 13.5 %shard_map.86.cnt = f32[128,512]{1,0:T(8,128)S(1)} custom-call(s32[128,1024]{1,0:T(8,128)S(1)} %copy-done), custom_call_target="tpu_custom_call" | custom-call | tf_op jit(solution)/shard_map/pallas_call | solution.py:344
  15.2 0.0 copy-done.1
  15.2 0.0 copy-done.2
  15.2 0.0 copy-done.3
  15.2 0.0 copy-done.4
  15.2 0.0 copy-done.5
  15.3 0.0 copy-done.6
  15.3 50.0 %shard_map.87 = (f32[1,128]{1,0:T(1,128)S(1)}, f32[256,256]{1,0:T(8,128)S(1)}) custom-call(bf16[128,256]{1,0:T(8,128)(2,1)S(1)} %copy-done.3, bf16[256,256]{1,0:T(8,128)(2,1)S(1)} %copy-done.2, bf16[12,128,128]{2,1,0:T(8,128)(2,1)S(1)} %copy-done.1, s32[12]{0:T(128)S(1)} %copy-done.6, s32[2,12]{1,0:T(2,128)S(1)} %copy-done.5, s32[2,256]{1,0:T(2,128)S(1)} %copy-done.4, ...), custom_call_target="tpu_custom_call" | custom-call | tf_op jit(solution)/shard_map/pallas_call | solution.py:356
  65.2 0.5 copy.11
  65.7 0.7 %copy.12 = f32[256,256]{1,0:T(8,128)} copy(f32[256,256]{1,0:T(8,128)S(1)} %get-tuple-element.9) | data formatting | bytes 524288
Async XLA Ops:
  0.6 1.0 %copy-start = (s32[128,1024]{1,0:T(8,128)S(1)}, s32[128,1024]{1,0:T(8,128)}, u32[]{:S(2)}) copy-start(s32[128,1024]{1,0:T(8,128)} %neg_ref.1) | copy-start | bytes 1572868
  1.7 13.5 %copy-start.1 = (bf16[12,128,128]{2,1,0:T(8,128)(2,1)S(1)}, bf16[12,128,128]{2,1,0:T(8,128)(2,1)}, u32[]{:S(2)}) copy-start(bf16[12,128,128]{2,1,0:T(8,128)(2,1)} %tiles.1) | copy-start | bytes 1179652
  1.7 13.5 %copy-start.2 = (bf16[256,256]{1,0:T(8,128)(2,1)S(1)}, bf16[256,256]{1,0:T(8,128)(2,1)}, u32[]{:S(2)}) copy-start(bf16[256,256]{1,0:T(8,128)(2,1)} %weight.1) | copy-start | bytes 393220
  1.7 13.5 %copy-start.3 = (bf16[128,256]{1,0:T(8,128)(2,1)S(1)}, bf16[128,256]{1,0:T(8,128)(2,1)}, u32[]{:S(2)}) copy-start(bf16[128,256]{1,0:T(8,128)(2,1)} %feat.1) | copy-start | bytes 196612
  1.7 13.6 %copy-start.4 = (s32[2,256]{1,0:T(2,128)S(1)}, s32[2,256]{1,0:T(2,128)}, u32[]{:S(2)}) copy-start(s32[2,256]{1,0:T(2,128)} %fkeep.1) | copy-start | bytes 6148
  1.7 13.6 %copy-start.5 = (s32[2,12]{1,0:T(2,128)S(1)}, s32[2,12]{1,0:T(2,128)}, u32[]{:S(2)}) copy-start(s32[2,12]{1,0:T(2,128)} %keep_ref.1) | copy-start | bytes 292
  1.7 13.6 %copy-start.6 = (s32[12]{0:T(128)S(1)}, s32[12]{0:T(128)}, u32[]{:S(2)}) copy-start(s32[12]{0:T(128)} %pos_ref.1) | copy-start | bytes 148

commit v2 on v1

--- a/solution.py
+++ b/solution.py
@@ -25,55 +25,70 @@
         lax.fori_loop(start, stop, step, 0)
 
 
-def count_kernel(neg_ref, cnt_ref):
-    rows, n_neg = neg_ref.shape
-    blocks = cnt_ref.shape[1] // 128
-    chunks = n_neg // 128
+def spread_matrix(ref):
+    n = ref.shape[0]
+    stride = n // 128
+    row = lax.broadcasted_iota(jnp.int32, (128, 128), 0)
+    lane = lax.broadcasted_iota(jnp.int32, (128, 128), 1)
+    for k in range(n // 128):
+        here = lane == row // stride + k * (128 // stride)
+        for s in range(stride):
+            hit = jnp.logical_and(here, row % stride == s)
+            ref[k * 128 : (k + 1) * 128, s * 128 : (s + 1) * 128] = jnp.where(hit, 1.0, 0.0).astype(BF16)
+
+
+def spread(neg, matrix, out):
+    low = (neg[...] & 255).astype(F32).astype(BF16)
+    high = (neg[...] >> 8).astype(F32).astype(BF16)
+    nodes = neg.shape[0]
+    both = jnp.dot(jnp.concatenate([low, high], axis=0), matrix[...], preferred_element_type=F32)
+    out[...] = (both[:nodes] + 256.0 * both[nodes:]).astype(jnp.int32)
+
+
+def count_rows(i, tall, spread_ref, cnt):
+    stride = spread_ref.shape[1] // 128
+    blocks = cnt.shape[1] // 128
     per = 4 if blocks % 4 == 0 else 1
-    lane = lax.broadcasted_iota(jnp.int32, (8, 128), 1)
-
-    def rank(parts, target):
-        total = jnp.zeros((8, 128), jnp.int32)
-        for part in parts:
-            low = jnp.zeros((8, 128), jnp.int32)
-            for step in (64, 32, 16, 8, 4, 2, 1):
-                seen = jnp.take_along_axis(part, low + (step - 1), axis=1, mode="promise_in_bounds")
-                low = jnp.where(seen <= target, low + step, low)
-            seen = jnp.take_along_axis(part, low, axis=1, mode="promise_in_bounds")
-            total = total + jnp.where(seen <= target, low + 1, low)
-        return total
-
-    def row_step(i, carry):
-        base = pl.multiple_of(i * 8, 8)
-        parts = [neg_ref[pl.ds(base, 8), k * 128 : (k + 1) * 128] for k in range(chunks)]
-
-        def block_step(g, before):
-            for j in range(per):
-                at = pl.multiple_of((g * per + j) * 128, 128)
-                now = rank(parts, lane + at)
-                rolled = pltpu.roll(now, 1, 1)
-                shifted = jnp.where(lane == 0, before, rolled)
-                cnt_ref[pl.ds(base, 8), pl.ds(at, 128)] = (now - shifted).astype(F32)
-                before = rolled
-            return before
-
-        first = jnp.zeros((8, 128), jnp.int32)
-        if blocks == per:
-            block_step(0, first)
-        else:
-            lax.fori_loop(0, blocks // per, block_step, first)
-        return carry
-
-    lax.fori_loop(0, rows // 8, row_step, 0)
+    rows = pl.ds(pl.multiple_of(i * tall, 8), tall)
+    lane = lax.broadcasted_iota(jnp.int32, (tall, 128), 1)
+
+    def take(part, index):
+        return jnp.take_along_axis(part, index, axis=1, mode="promise_in_bounds")
+
+    def block_step(g, before):
+        starts = [pl.multiple_of((g * per + j) * 128, 128) for j in range(per)]
+        targets = [lane + at for at in starts]
+        last = spread_ref[rows, (stride - 1) * 128 : stride * 128]
+        lows = [jnp.zeros((tall, 128), jnp.int32)] * per
+        for step in (64, 32, 16, 8, 4, 2, 1):
+            seen = [take(last, low + (step - 1)) for low in lows]
+            lows = [jnp.where(x <= t, low + step, low) for x, t, low in zip(seen, targets, lows)]
+        ranks = [low * stride for low in lows]
+        for s in range(stride):
+            part = spread_ref[rows, s * 128 : (s + 1) * 128]
+            seen = [take(part, low) for low in lows]
+            ranks = [jnp.where(x <= t, k + 1, k) for x, t, k in zip(seen, targets, ranks)]
+        for at, now in zip(starts, ranks):
+            rolled = pltpu.roll(now, 1, 1)
+            cnt[rows, pl.ds(at, 128)] = (now - jnp.where(lane == 0, before, rolled)).astype(F32)
+            before = rolled
+        return before
+
+    first = jnp.zeros((tall, 128), jnp.int32)
+    if blocks == per:
+        block_step(0, first)
+    else:
+        lax.fori_loop(0, blocks // per, block_step, first)
 
 
 def step_kernel(
     R, C,
-    feat, weight, tiles, pos_ref, keep_ref, fkeep, cnt,
+    feat, weight_in, tiles_in, pos_ref, keep_ref, fkeep, neg_in,
     loss_out, grad_out,
+    weight, tiles, neg, matrix, spread_ref, cnt,
     xg, xcat, pbuf, rbuf, gbuf, embf, embb, rinv, eb, wacc, wbuf, wr, ws, wc, wd, obuf,
     f_send, f_recv, s_send, s_recv, p_send, p_recv, g_send, g_recv,
-    a_send, a_recv, b_send, b_recv, c_send, c_recv, d_send, d_recv,
+    a_send, a_recv, b_send, b_recv, c_send, c_recv, d_send, d_recv, l_sem,
 ):
     nodes, width = feat.shape
     slots = tiles.shape[0]
@@ -104,6 +119,15 @@
             device_id=(r, c), device_id_type=MESH,
         )
 
+    loads = [
+        pltpu.make_async_copy(neg_in, neg, l_sem.at[0]),
+        pltpu.make_async_copy(tiles_in, tiles, l_sem.at[1]),
+        pltpu.make_async_copy(weight_in, weight, l_sem.at[2]),
+        pltpu.make_async_copy(feat, xg.at[me_c], l_sem.at[3]),
+    ]
+    for load in loads:
+        load.start()
+
     barrier = pltpu.get_barrier_semaphore()
     loop(1, R, lambda o: pl.semaphore_signal(barrier, inc=1, device_id=(at_row(o), me_c), device_id_type=MESH))
     loop(1, C, lambda o: pl.semaphore_signal(barrier, inc=1, device_id=(me_r, at_col(o)), device_id_type=MESH))
@@ -121,7 +145,11 @@
 
     loop(1, chips, lambda o: far(o).start())
     near(0).start()
-    xg[me_c] = feat[...]
+    spread_matrix(matrix)
+    loads[0].wait()
+    spread(neg, matrix, spread_ref)
+    tall = 32
+    turns = nodes // tall
 
     def pass_on(o):
         far(o).wait_recv()
@@ -130,6 +158,8 @@
     loop(1, chips, pass_on)
     near(0).wait_recv()
     loop(1, chips, lambda o: near(o).wait_recv())
+    loads[3].wait()
+    loads[1].wait()
 
     where = [jnp.maximum(pos_ref[k], 0) for k in range(slots)]
     trow = [w // C for w in where]
@@ -161,6 +191,9 @@
     mine = part(0)
     pbuf[0, 0] = mine[0]
     pbuf[0, 1] = mine[1]
+    for i in range(turns):
+        count_rows(i, tall, spread_ref, cnt)
+    loads[2].wait()
     loop(1, R, lambda o: part_copy(o).wait_recv())
 
     for v in range(2):
@@ -341,16 +374,10 @@
     C = lax.axis_size("col")
     group = R * nodes
     chips = C // 2
-    counts = pl.pallas_call(
-        count_kernel,
-        out_shape=jax.ShapeDtypeStruct((nodes, group), F32),
-        in_specs=[pl.BlockSpec(memory_space=pltpu.VMEM)],
-        out_specs=pl.BlockSpec(memory_space=pltpu.VMEM),
-        compiler_params=pltpu.CompilerParams(vmem_limit_bytes=16 << 20),
-    )(negatives)
     cr = up(width, R, 8)
     cc = up(cr, C, 8)
     vmem = pl.BlockSpec(memory_space=pltpu.VMEM)
+    held = pl.BlockSpec(memory_space=pl.ANY)
     smem = pl.BlockSpec(memory_space=pltpu.SMEM)
     sem = pltpu.SemaphoreType.DMA
     loss, grad = pl.pallas_call(
@@ -359,9 +386,15 @@
             jax.ShapeDtypeStruct((1, nodes), F32),
             jax.ShapeDtypeStruct((width, width), F32),
         ),
-        in_specs=[vmem, vmem, vmem, smem, smem, vmem, vmem],
+        in_specs=[held, held, held, smem, smem, vmem, held],
         out_specs=(vmem, vmem),
         scratch_shapes=[
+            pltpu.VMEM(weight.shape, BF16),
+            pltpu.VMEM(tiles.shape, BF16),
+            pltpu.VMEM(negatives.shape, jnp.int32),
+            pltpu.VMEM((negatives.shape[1], negatives.shape[1]), BF16),
+            pltpu.VMEM(negatives.shape, jnp.int32),
+            pltpu.VMEM((nodes, group), F32),
             pltpu.VMEM((C, nodes, width), BF16),
             pltpu.VMEM((slots * 128, width), BF16),
             pltpu.VMEM((R, 2, nodes, width), BF16),
@@ -381,12 +414,12 @@
             sem((chips,)), sem((chips,)), sem((chips,)), sem((chips,)),
             sem((R,)), sem((R,)), sem((R,)), sem((R,)),
             sem((R,)), sem((R,)), sem((C,)), sem((C,)),
-            sem((C,)), sem((C,)), sem((R,)), sem((R,)),
+            sem((C,)), sem((C,)), sem((R,)), sem((R,)), sem((4,)),
         ],
         compiler_params=pltpu.CompilerParams(
             collective_id=0, has_side_effects=True, vmem_limit_bytes=48 << 20
         ),
-    )(features, weight, tiles, tile_pos, edge_keep, feature_keep, counts)
+    )(features, weight, tiles, tile_pos, edge_keep, feature_keep, negatives)
     return loss.reshape(nodes), grad
 
 

time: 66.6 us -> 58.2 us (0.87)
  Pallas kernels: 63.5 us -> 50.2 us
  local copies, waits for them, and re-layouts: 2.27 us -> 7 us
    pallas_call x1 -> x0, Pallas kernels: 13.5 us -> none  [shards(): pl.pallas_call(count_kernel, out_shape=jax.ShapeDtypeStruct((nodes, group...]
    unnamed x16, local copies, waits for them, and re-layouts: 2.27 us -> 7 us
where the time goes in v2:
time: 58.2 us; the launch traced here: 57.9 us
  Pallas kernels  50.2 us (86%)
  local copies, waits for them, and re-layouts  7 us (12%)
  between operations  0.66 us (1%)
    pallas_call x1, Pallas kernels, shards(): pl.pallas_call(functools.partial(step_kernel, R, C), out_shape=(jax.Shape...  50.2 us
    unnamed x16, local copies, waits for them, and re-layouts  7 us

profile of v2, /device:TPU:0, one launch (start us, length us, event | category | flops | bytes accessed | tf_op | source)
XLA Modules:
  0.0 57.9 jit_solution(7782690570600844618)
XLA Ops:
  0.6 0.0 copy-start
  0.6 1.0 %copy-done = s32[128,1024]{1,0:T(8,128)S(1)} copy-done((s32[128,1024]{1,0:T(8,128)S(1)}, s32[128,1024]{1,0:T(8,128)}, u32[]{:S(2)}) %copy-start) | copy-done | bytes 524312
  1.7 0.0 copy-start.1
  1.7 1.0 %copy-done.1 = bf16[12,128,128]{2,1,0:T(8,128)(2,1)S(1)} copy-done((bf16[12,128,128]{2,1,0:T(8,128)(2,1)S(1)}, bf16[12,128,128]{2,1,0:T(8,128)(2,1)}, u32[]{:S(2)}) %copy-start.1) | copy-done | bytes 393240
  2.7 0.0 copy-start.2
  2.7 0.9 %copy-done.2 = bf16[256,256]{1,0:T(8,128)(2,1)S(1)} copy-done((bf16[256,256]{1,0:T(8,128)(2,1)S(1)}, bf16[256,256]{1,0:T(8,128)(2,1)}, u32[]{:S(2)}) %copy-start.2) | copy-done | bytes 131096
  3.6 0.0 copy-start.3
  3.6 0.8 %copy-done.3 = bf16[128,256]{1,0:T(8,128)(2,1)S(1)} copy-done((bf16[128,256]{1,0:T(8,128)(2,1)S(1)}, bf16[128,256]{1,0:T(8,128)(2,1)}, u32[]{:S(2)}) %copy-start.3) | copy-done | bytes 65560
  4.4 0.0 copy-start.4
  4.4 0.7 %copy-done.4 = s32[2,256]{1,0:T(2,128)S(1)} copy-done((s32[2,256]{1,0:T(2,128)S(1)}, s32[2,256]{1,0:T(2,128)}, u32[]{:S(2)}) %copy-start.4) | copy-done | bytes 2072
  5.1 0.0 copy-start.5
  5.1 0.7 %copy-done.5 = s32[2,12]{1,0:T(2,128)S(1)} copy-done((s32[2,12]{1,0:T(2,128)S(1)}, s32[2,12]{1,0:T(2,128)}, u32[]{:S(2)}) %copy-start.5) | copy-done | bytes 120
  5.8 0.0 copy-start.6
  5.8 0.7 %copy-done.6 = s32[12]{0:T(128)S(1)} copy-done((s32[12]{0:T(128)S(1)}, s32[12]{0:T(128)}, u32[]{:S(2)}) %copy-start.6) | copy-done | bytes 72
  6.4 50.2 %shard_map.86 = (f32[1,128]{1,0:T(1,128)S(1)}, f32[256,256]{1,0:T(8,128)S(1)}) custom-call(bf16[128,256]{1,0:T(8,128)(2,1)S(1)} %copy-done.3, bf16[256,256]{1,0:T(8,128)(2,1)S(1)} %copy-done.2, bf16[12,128,128]{2,1,0:T(8,128)(2,1)S(1)} %copy-done.1, s32[12]{0:T(128)S(1)} %copy-done.6, s32[2,12]{1,0:T(2,128)S(1)} %copy-done.5, s32[2,256]{1,0:T(2,128)S(1)} %copy-done.4, ...), custom_call_target="tpu_custom_call" | custom-call | tf_op jit(solution)/shard_map/pallas_call | solution.py:383
  56.7 0.5 copy.11
  57.2 0.7 %copy.12 = f32[256,256]{1,0:T(8,128)} copy(f32[256,256]{1,0:T(8,128)S(1)} %get-tuple-element.9) | data formatting | bytes 524288
Async XLA Ops:
  0.6 1.0 %copy-start = (s32[128,1024]{1,0:T(8,128)S(1)}, s32[128,1024]{1,0:T(8,128)}, u32[]{:S(2)}) copy-start(s32[128,1024]{1,0:T(8,128)} %neg_in.1) | copy-start | bytes 1572868
  1.7 1.0 %copy-start.1 = (bf16[12,128,128]{2,1,0:T(8,128)(2,1)S(1)}, bf16[12,128,128]{2,1,0:T(8,128)(2,1)}, u32[]{:S(2)}) copy-start(bf16[12,128,128]{2,1,0:T(8,128)(2,1)} %tiles_in.1) | copy-start | bytes 1179652
  2.7 0.9 %copy-start.2 = (bf16[256,256]{1,0:T(8,128)(2,1)S(1)}, bf16[256,256]{1,0:T(8,128)(2,1)}, u32[]{:S(2)}) copy-start(bf16[256,256]{1,0:T(8,128)(2,1)} %weight_in.1) | copy-start | bytes 393220
  3.6 0.8 %copy-start.3 = (bf16[128,256]{1,0:T(8,128)(2,1)S(1)}, bf16[128,256]{1,0:T(8,128)(2,1)}, u32[]{:S(2)}) copy-start(bf16[128,256]{1,0:T(8,128)(2,1)} %feat.1) | copy-start | bytes 196612
  4.4 0.7 %copy-start.4 = (s32[2,256]{1,0:T(2,128)S(1)}, s32[2,256]{1,0:T(2,128)}, u32[]{:S(2)}) copy-start(s32[2,256]{1,0:T(2,128)} %fkeep.1) | copy-start | bytes 6148
  5.1 0.7 %copy-start.5 = (s32[2,12]{1,0:T(2,128)S(1)}, s32[2,12]{1,0:T(2,128)}, u32[]{:S(2)}) copy-start(s32[2,12]{1,0:T(2,128)} %keep_ref.1) | copy-start | bytes 292
  5.8 0.7 %copy-start.6 = (s32[12]{0:T(128)S(1)}, s32[12]{0:T(128)}, u32[]{:S(2)}) copy-start(s32[12]{0:T(128)} %pos_ref.1) | copy-start | bytes 148

commit v3 on v2

--- a/solution.py
+++ b/solution.py
@@ -86,11 +86,12 @@
     feat, weight_in, tiles_in, pos_ref, keep_ref, fkeep, neg_in,
     loss_out, grad_out,
     weight, tiles, neg, matrix, spread_ref, cnt,
-    xg, xcat, pbuf, rbuf, gbuf, embf, embb, rinv, eb, wacc, wbuf, wr, ws, wc, wd, obuf,
+    xg, prod, pbuf, rbuf, gbuf, embf, embb, rinv, eb, wacc, wbuf, wr, ws, wc, wd, obuf,
     f_send, f_recv, s_send, s_recv, p_send, p_recv, g_send, g_recv,
     a_send, a_recv, b_send, b_recv, c_send, c_recv, d_send, d_recv, l_sem,
 ):
     nodes, width = feat.shape
+    halves = width // 128
     slots = tiles.shape[0]
     chips = C // 2
     cr = wr.shape[1]
@@ -123,8 +124,9 @@
         pltpu.make_async_copy(neg_in, neg, l_sem.at[0]),
         pltpu.make_async_copy(tiles_in, tiles, l_sem.at[1]),
         pltpu.make_async_copy(weight_in, weight, l_sem.at[2]),
-        pltpu.make_async_copy(feat, xg.at[me_c], l_sem.at[3]),
     ]
+    for h in range(halves):
+        loads.append(pltpu.make_async_copy(feat.at[:, h * 128 : (h + 1) * 128], xg[h].at[me_c], l_sem.at[3 + h]))
     for load in loads:
         load.start()
 
@@ -133,83 +135,84 @@
     loop(1, C, lambda o: pl.semaphore_signal(barrier, inc=1, device_id=(me_r, at_col(o)), device_id_type=MESH))
     pl.semaphore_wait(barrier, R + C - 2)
 
-    def far(o):
+    def far(h, o):
         to = lax.rem(chip + o, chips) * 2 + core
-        return copy(feat, xg.at[me_c], f_send.at[o], f_recv.at[o], me_r, to)
-
-    def near(o):
+        return copy(feat.at[:, h * 128 : (h + 1) * 128], xg[h].at[me_c], f_send.at[h, o], f_recv.at[h, o], me_r, to)
+
+    def near(h, o):
         if isinstance(o, int) and o == 0:
-            return copy(feat, xg.at[me_c], s_send.at[0], s_recv.at[0], me_r, sib)
+            return copy(feat.at[:, h * 128 : (h + 1) * 128], xg[h].at[me_c], s_send.at[h, 0], s_recv.at[h, 0], me_r, sib)
         slot = lax.rem(chip + chips - o, chips) * 2 + core
-        return copy(xg.at[slot], xg.at[slot], s_send.at[o], s_recv.at[o], me_r, sib)
-
-    loop(1, chips, lambda o: far(o).start())
-    near(0).start()
+        return copy(xg[h].at[slot], xg[h].at[slot], s_send.at[h, o], s_recv.at[h, o], me_r, sib)
+
+    for h in range(halves):
+        loop(1, chips, lambda o: far(h, o).start())
+        near(h, 0).start()
     spread_matrix(matrix)
     loads[0].wait()
     spread(neg, matrix, spread_ref)
     tall = 32
     turns = nodes // tall
-
-    def pass_on(o):
-        far(o).wait_recv()
-        near(o).start()
-
-    loop(1, chips, pass_on)
-    near(0).wait_recv()
-    loop(1, chips, lambda o: near(o).wait_recv())
-    loads[3].wait()
-    loads[1].wait()
+    for i in range(turns // 2):
+        count_rows(i, tall, spread_ref, cnt)
 
     where = [jnp.maximum(pos_ref[k], 0) for k in range(slots)]
     trow = [w // C for w in where]
     live = [[keep_ref[v, k] * (pos_ref[k] >= 0).astype(jnp.int32) for k in range(slots)] for v in range(2)]
-    for k in range(slots):
-        xcat[k * 128 : (k + 1) * 128, :] = xg[lax.rem(where[k], C)]
-
-    def part_copy(o):
-        return copy(pbuf.at[o], rbuf.at[o], p_send.at[o], p_recv.at[o], at_row(o), me_c)
-
-    def part(o):
+
+    def part_copy(h, o):
+        return copy(pbuf.at[h, o], rbuf.at[h, o], p_send.at[h, o], p_recv.at[h, o], at_row(o), me_c)
+
+    def part(h, o):
         t = at_row(o)
-        out = []
+        here = [trow[k] == t for k in range(slots)]
         for v in range(2):
-            lhs = []
+            total = None
             for k in range(slots):
-                use = jnp.where(trow[k] == t, live[v][k], 0).astype(F32)
-                lhs.append(tiles[k] * jnp.full((1, 128), use, F32).astype(BF16))
-            out.append(jnp.dot(jnp.concatenate(lhs, axis=1), xcat[...], preferred_element_type=F32).astype(BF16))
-        return out
-
-    def part_send(o):
-        first, second = part(o)
-        pbuf[o, 0] = first
-        pbuf[o, 1] = second
-        part_copy(o).start()
-
-    loop(1, R, part_send)
-    mine = part(0)
-    pbuf[0, 0] = mine[0]
-    pbuf[0, 1] = mine[1]
-    for i in range(turns):
+                term = prod[k] * jnp.where(here[k], live[v][k], 0).astype(F32)
+                total = term if total is None else total + term
+            pbuf[h, o, v] = total.astype(BF16)
+
+    for h in range(halves):
+        def pass_on(o):
+            far(h, o).wait_recv()
+            near(h, o).start()
+
+        loop(1, chips, pass_on)
+        near(h, 0).wait_recv()
+        loop(1, chips, lambda o: near(h, o).wait_recv())
+        loads[3 + h].wait()
+        if h == 0:
+            loads[1].wait()
+        for k in range(slots):
+            prod[k] = jnp.dot(tiles[k], xg[h][lax.rem(where[k], C)], preferred_element_type=F32)
+
+        def part_send(o):
+            part(h, o)
+            part_copy(h, o).start()
+
+        loop(1, R, part_send)
+        part(h, 0)
+
+    def agg_copy(h, o):
+        ref = gbuf.at[me_r, :, :, h * 128 : (h + 1) * 128]
+        return copy(ref, ref, g_send.at[h, o], g_recv.at[h, o], at_row(o), me_c)
+
+    for h in range(halves):
+        loop(1, R, lambda o: part_copy(h, o).wait_recv())
+        for v in range(2):
+            total = pbuf[h, 0, v].astype(F32)
+            if R <= 8:
+                for o in range(1, R):
+                    total = total + rbuf[h, o, v].astype(F32)
+            else:
+                total = lax.fori_loop(1, R, lambda o, acc: acc + rbuf[h, o, v].astype(F32), total)
+            total = total * fkeep[v : v + 1, h * 128 : (h + 1) * 128].astype(F32)
+            gbuf[me_r, v, :, h * 128 : (h + 1) * 128] = total.astype(BF16)
+        loop(1, R, lambda o: agg_copy(h, o).start())
+    for i in range(turns // 2, turns):
         count_rows(i, tall, spread_ref, cnt)
     loads[2].wait()
-    loop(1, R, lambda o: part_copy(o).wait_recv())
-
-    for v in range(2):
-        total = pbuf[0, v].astype(F32)
-        if R <= 8:
-            for o in range(1, R):
-                total = total + rbuf[o, v].astype(F32)
-        else:
-            total = lax.fori_loop(1, R, lambda o, acc: acc + rbuf[o, v].astype(F32), total)
-        total = total * fkeep[v : v + 1, :].astype(F32)
-        gbuf[me_r, v] = total.astype(BF16)
-
-    def agg_copy(o):
-        return copy(gbuf.at[me_r], gbuf.at[me_r], g_send.at[o], g_recv.at[o], at_row(o), me_c)
-
-    loop(1, R, lambda o: agg_copy(o).start())
 
     def embed(r):
         for v in range(2):
@@ -241,7 +244,8 @@
 
     def arrived(o):
         r = from_row(o)
-        agg_copy(o).wait_recv()
+        for h in range(halves):
+            agg_copy(h, o).wait_recv()
         embed(r)
         scores(r)
 
@@ -260,7 +264,7 @@
     tot1 = epos + row_sum(0)
     tot2 = epos + row_sum(1)
     loss = 0.5 * (jnp.log(tot1) - pos + (jnp.log(tot2) - pos))
-    loss_out[...] = jnp.broadcast_to(loss, (nodes, 128)).T[0:1, :]
+    loss_out[...] = jnp.broadcast_to(loss, (nodes, 128)).T[0]
     both = epos / tot1 + epos / tot2 - 2.0
     coef = 1.0 / (2.0 * tau * float(R * C * nodes) ** 0.5)
 
@@ -352,11 +356,12 @@
     loop(1, R, lambda o: d_copy(o).wait_recv())
     grad_out[...] = obuf[0:width, :]
 
-    loop(1, chips, lambda o: far(o).wait_send())
-    near(0).wait_send()
-    loop(1, chips, lambda o: near(o).wait_send())
-    loop(1, R, lambda o: part_copy(o).wait_send())
-    loop(1, R, lambda o: agg_copy(o).wait_send())
+    for h in range(halves):
+        loop(1, chips, lambda o: far(h, o).wait_send())
+        near(h, 0).wait_send()
+        loop(1, chips, lambda o: near(h, o).wait_send())
+        loop(1, R, lambda o: part_copy(h, o).wait_send())
+        loop(1, R, lambda o: agg_copy(h, o).wait_send())
     loop(1, R, lambda o: a_copy(o).wait_send())
     loop(1, C, lambda o: b_copy(o).wait_send())
     loop(1, C, lambda o: c_copy(o).wait_send())
@@ -369,6 +374,7 @@
 
 def shards(features, weight, tiles, tile_pos, edge_keep, feature_keep, negatives):
     nodes, width = features.shape
+    halves = width // 128
     slots = tiles.shape[0]
     R = lax.axis_size("row")
     C = lax.axis_size("col")
@@ -383,7 +389,7 @@
     loss, grad = pl.pallas_call(
         functools.partial(step_kernel, R, C),
         out_shape=(
-            jax.ShapeDtypeStruct((1, nodes), F32),
+            jax.ShapeDtypeStruct((nodes,), F32),
             jax.ShapeDtypeStruct((width, width), F32),
         ),
         in_specs=[held, held, held, smem, smem, vmem, held],
@@ -395,10 +401,10 @@
             pltpu.VMEM((negatives.shape[1], negatives.shape[1]), BF16),
             pltpu.VMEM(negatives.shape, jnp.int32),
             pltpu.VMEM((nodes, group), F32),
-            pltpu.VMEM((C, nodes, width), BF16),
-            pltpu.VMEM((slots * 128, width), BF16),
-            pltpu.VMEM((R, 2, nodes, width), BF16),
-            pltpu.VMEM((R, 2, nodes, width), BF16),
+            [pltpu.VMEM((C, nodes, 128), BF16)] * halves,
+            pltpu.VMEM((slots, 128, 128), F32),
+            pltpu.VMEM((halves, R, 2, nodes, 128), BF16),
+            pltpu.VMEM((halves, R, 2, nodes, 128), BF16),
             pltpu.VMEM((R, 2, nodes, width), BF16),
             pltpu.VMEM((R, 2, nodes, width), F32),
             pltpu.VMEM((R, 2, nodes, width), BF16),
@@ -411,16 +417,16 @@
             pltpu.VMEM((C, cc, width), F32),
             pltpu.VMEM((C * cc, width), F32),
             pltpu.VMEM((R * cr, width), F32),
-            sem((chips,)), sem((chips,)), sem((chips,)), sem((chips,)),
-            sem((R,)), sem((R,)), sem((R,)), sem((R,)),
+            sem((halves, chips)), sem((halves, chips)), sem((halves, chips)), sem((halves, chips)),
+            sem((halves, R)), sem((halves, R)), sem((halves, R)), sem((halves, R)),
             sem((R,)), sem((R,)), sem((C,)), sem((C,)),
-            sem((C,)), sem((C,)), sem((R,)), sem((R,)), sem((4,)),
+            sem((C,)), sem((C,)), sem((R,)), sem((R,)), sem((3 + halves,)),
         ],
         compiler_params=pltpu.CompilerParams(
-            collective_id=0, has_side_effects=True, vmem_limit_bytes=48 << 20
+            collective_id=0, has_side_effects=True, vmem_limit_bytes=60 << 20
         ),
     )(features, weight, tiles, tile_pos, edge_keep, feature_keep, negatives)
-    return loss.reshape(nodes), grad
+    return loss, grad
 
 
 def solution(mesh):

time: 58.2 us -> 51.5 us (0.88)
  local copies, waits for them, and re-layouts: 7 us -> 2.74 us
  Pallas kernels: 50.2 us -> 47.9 us
    unnamed x16 -> x4, local copies, waits for them, and re-layouts: 7 us -> 2.74 us
    pallas_call x1, Pallas kernels: 50.2 us -> 47.9 us  [shards(): pl.pallas_call(functools.partial(step_kernel, R, C), out_shape=(jax.Shape...]
where the time goes in v3:
time: 51.5 us; the launch traced here: 51.3 us
  Pallas kernels  47.9 us (93%)
  local copies, waits for them, and re-layouts  2.74 us (5%)
  between operations  0.65 us (1%)
    pallas_call x1, Pallas kernels, shards(): pl.pallas_call(functools.partial(step_kernel, R, C), out_shape=(jax.Shape...  47.9 us
    unnamed x4, local copies, waits for them, and re-layouts  2.74 us

profile of v3, /device:TPU:0, one launch (start us, length us, event | category | flops | bytes accessed | tf_op | source)
XLA Modules:
  0.0 51.3 jit_solution(17854270241995335058)
XLA Ops:
  0.6 47.9 %shard_map.86 = (f32[128]{0:T(128)}, f32[256,256]{1,0:T(8,128)}) custom-call(bf16[128,256]{1,0:T(8,128)(2,1)} %feat.1, bf16[256,256]{1,0:T(8,128)(2,1)} %weight_in.1, bf16[12,128,128]{2,1,0:T(8,128)(2,1)} %tiles_in.1, s32[12]{0:T(128)} %pos_ref.1, s32[2,12]{1,0:T(2,128)} %keep_ref.1, s32[2,256]{1,0:T(2,128)} %fkeep.1, s32[128,1024]{1,0:T(8,128)} %neg_in.1), custom_call_target="tpu_custom_call" | custom-call | tf_op jit(solution)/shard_map/pallas_call | solution.py:389
  48.6 0.0 copy-start
  48.6 0.6 %copy-done = f32[128]{0:T(128)S(1)} copy-done((f32[128]{0:T(128)S(1)}, f32[128]{0:T(128)}, u32[]{:S(2)}) %copy-start) | copy-done | bytes 536
  49.1 0.5 copy.11
  49.6 1.7 %copy.12 = f32[256,256]{1,0:T(8,128)} copy(f32[256,256]{1,0:T(8,128)} %get-tuple-element.5) | data formatting | bytes 524288
Async XLA Ops:
  48.6 0.6 %copy-start = (f32[128]{0:T(128)S(1)}, f32[128]{0:T(128)}, u32[]{:S(2)}) copy-start(f32[128]{0:T(128)} %get-tuple-element.4) | copy-start | bytes 1540

commit v4 on v3

--- a/solution.py
+++ b/solution.py
@@ -15,7 +15,7 @@
 
 
 def loop(start, stop, body):
-    if stop - start <= 8:
+    if stop - start <= 16:
         for i in range(start, stop):
             body(i)
     else:
@@ -83,10 +83,10 @@
 
 def step_kernel(
     R, C,
-    feat, weight_in, tiles_in, pos_ref, keep_ref, fkeep, neg_in,
+    feat, weight_in, tiles_in, pos_in, keep_in, fkeep_in, neg_in,
     loss_out, grad_out,
-    weight, tiles, neg, matrix, spread_ref, cnt,
-    xg, prod, pbuf, rbuf, gbuf, embf, embb, rinv, eb, wacc, wbuf, wr, ws, wc, wd, obuf,
+    weight, tiles, pos_ref, keep_ref, fkeep, neg, matrix, spread_ref, cnt,
+    xg, prod, pbuf, rbuf, gbuf, embf, embb, rinv, eb, turned, dzb, wbuf, wsib, whalf, wr, obuf,
     f_send, f_recv, s_send, s_recv, p_send, p_recv, g_send, g_recv,
     a_send, a_recv, b_send, b_recv, c_send, c_recv, d_send, d_recv, l_sem,
 ):
@@ -94,8 +94,8 @@
     halves = width // 128
     slots = tiles.shape[0]
     chips = C // 2
-    cr = wr.shape[1]
-    cc = wc.shape[1]
+    peers = R * chips
+    piece_rows = wr.shape[1]
     me_r = lax.axis_index("row")
     me_c = lax.axis_index("col")
     chip = me_c // 2
@@ -108,11 +108,11 @@
     def from_row(o):
         return lax.rem(me_r + R - o, R)
 
-    def at_col(o):
-        return lax.rem(me_c + o, C)
-
-    def from_col(o):
-        return lax.rem(me_c + C - o, C)
+    index = me_r * chips + chip
+
+    def at_peer(o):
+        to = lax.rem(index + o, peers)
+        return to // chips, lax.rem(to, chips) * 2 + core
 
     def copy(src, dst, send, recv, r, c):
         return pltpu.make_async_remote_copy(
@@ -127,13 +127,16 @@
     ]
     for h in range(halves):
         loads.append(pltpu.make_async_copy(feat.at[:, h * 128 : (h + 1) * 128], xg[h].at[me_c], l_sem.at[3 + h]))
+    loads.append(pltpu.make_async_copy(pos_in, pos_ref, l_sem.at[3 + halves]))
+    loads.append(pltpu.make_async_copy(keep_in, keep_ref, l_sem.at[4 + halves]))
+    loads.append(pltpu.make_async_copy(fkeep_in, fkeep, l_sem.at[5 + halves]))
     for load in loads:
         load.start()
 
     barrier = pltpu.get_barrier_semaphore()
-    loop(1, R, lambda o: pl.semaphore_signal(barrier, inc=1, device_id=(at_row(o), me_c), device_id_type=MESH))
-    loop(1, C, lambda o: pl.semaphore_signal(barrier, inc=1, device_id=(me_r, at_col(o)), device_id_type=MESH))
-    pl.semaphore_wait(barrier, R + C - 2)
+    loop(1, peers, lambda o: pl.semaphore_signal(barrier, inc=1, device_id=at_peer(o), device_id_type=MESH))
+    pl.semaphore_signal(barrier, inc=1, device_id=(me_r, sib), device_id_type=MESH)
+    pl.semaphore_wait(barrier, peers)
 
     def far(h, o):
         to = lax.rem(chip + o, chips) * 2 + core
@@ -156,6 +159,8 @@
     for i in range(turns // 2):
         count_rows(i, tall, spread_ref, cnt)
 
+    for load in loads[3 + halves :]:
+        load.wait()
     where = [jnp.maximum(pos_ref[k], 0) for k in range(slots)]
     trow = [w // C for w in where]
     live = [[keep_ref[v, k] * (pos_ref[k] >= 0).astype(jnp.int32) for k in range(slots)] for v in range(2)]
@@ -215,13 +220,14 @@
     loads[2].wait()
 
     def embed(r):
-        for v in range(2):
-            z = jnp.dot(gbuf[r, v], weight[...], preferred_element_type=F32)
-            scale = lax.rsqrt(jnp.sum(z * z, -1, keepdims=True) + eps)
-            emb = z * scale
-            rinv[r, v] = scale
-            embf[r, v] = emb
-            embb[r, v] = emb.astype(BF16)
+        stacked = gbuf[r].reshape(2 * nodes, width)
+        z = jnp.dot(stacked, weight[...], preferred_element_type=F32)
+        scale = lax.rsqrt(jnp.sum(z * z, -1, keepdims=True) + eps)
+        emb = z * scale
+        rinv[r] = scale.reshape(2, nodes, 1)
+        embf[r] = emb.reshape(2, nodes, width)
+        embb[r] = emb.astype(BF16).reshape(2, nodes, width)
+        turned[r] = stacked.T
 
     embed(me_r)
     h1 = embb[me_r, 0]
@@ -269,16 +275,12 @@
     coef = 1.0 / (2.0 * tau * float(R * C * nodes) ** 0.5)
 
     def dz_term(r, d_one, d_two):
-        parts = []
         for v, d in enumerate((d_one, d_two)):
             emb = embf[r, v]
             dz = (d - emb * jnp.sum(emb * d, -1, keepdims=True)) * rinv[r, v]
             high = dz.astype(BF16)
-            low = (dz - high.astype(F32)).astype(BF16)
-            parts.append(jnp.concatenate([high, low], axis=1))
-        rhs = jnp.concatenate(parts, axis=0)
-        lhs = jnp.concatenate([gbuf[r, 0], gbuf[r, 1]], axis=0)
-        return lax.dot_general(lhs, rhs, TN, preferred_element_type=F32)
+            dzb[r, v * nodes : (v + 1) * nodes, :width] = high
+            dzb[r, v * nodes : (v + 1) * nodes, width:] = (dz - high.astype(F32)).astype(BF16)
 
     def weights(r):
         q1 = (eb[r, 0] / tot1).astype(BF16)
@@ -290,12 +292,11 @@
         return fore1, fore2, back1, back2
 
     acc1, acc2, own1, own2 = weights(me_r)
-    wacc[...] = jnp.zeros_like(wacc)
 
     def other(o, carry):
         r = from_row(o)
         fore1, fore2, back1, back2 = weights(r)
-        wacc[...] += dz_term(r, coef * back1, coef * back2)
+        dz_term(r, coef * back1, coef * back2)
         return carry[0] + fore1, carry[1] + fore2
 
     if R <= 8:
@@ -303,58 +304,64 @@
             acc1, acc2 = other(o, (acc1, acc2))
     else:
         acc1, acc2 = lax.fori_loop(1, R, other, (acc1, acc2))
-    both_terms = wacc[...] + dz_term(
+    dz_term(
         me_r, coef * (both * h2f + acc1 + own1), coef * (both * h1f + acc2 + own2)
     )
-    if wbuf.shape[0] > width:
-        wbuf[...] = jnp.zeros_like(wbuf)
-    wbuf[0:width, :] = both_terms[:, :width] + both_terms[:, width:]
-
-    def a_copy(o):
-        rows = pl.ds(pl.multiple_of(at_row(o) * cr, 8), cr)
-        return copy(wbuf.at[rows, :], wr.at[o], a_send.at[o], a_recv.at[o], at_row(o), me_c)
-
-    loop(1, R, lambda o: a_copy(o).start())
-    own = wbuf[pl.ds(pl.multiple_of(me_r * cr, 8), cr), :]
-    if ws.shape[0] > cr:
-        ws[...] = jnp.zeros_like(ws)
-    loop(1, R, lambda o: a_copy(o).wait_recv())
+
+    def grad_term(r):
+        return jnp.dot(turned[r], dzb[r], preferred_element_type=F32)
+
     if R <= 8:
-        for o in range(1, R):
-            own = own + wr[o]
+        terms = grad_term(0)
+        for r in range(1, R):
+            terms = terms + grad_term(r)
     else:
-        own = lax.fori_loop(1, R, lambda o, acc: acc + wr[o], own)
-    ws[0:cr, :] = own
+        terms = lax.fori_loop(1, R, lambda r, acc: acc + grad_term(r), grad_term(0))
+    wbuf[...] = terms[:, :width] + terms[:, width:]
+
+    half = width // 2
+    a_copy = copy(
+        wbuf.at[pl.ds(pl.multiple_of((1 - core) * half, 8), half), :], wsib, a_send, a_recv, me_r, sib
+    )
+    a_copy.start()
+    own = wbuf[pl.ds(pl.multiple_of(core * half, 8), half), :]
+    if whalf.shape[0] > half:
+        whalf[...] = jnp.zeros_like(whalf)
+    a_copy.wait_recv()
+    whalf[0:half, :] = own + wsib[...]
 
     def b_copy(o):
-        rows = pl.ds(pl.multiple_of(at_col(o) * cc, 8), cc)
-        return copy(ws.at[rows, :], wc.at[o], b_send.at[o], b_recv.at[o], me_r, at_col(o))
-
-    loop(1, C, lambda o: b_copy(o).start())
-    piece = ws[pl.ds(pl.multiple_of(me_c * cc, 8), cc), :]
-    loop(1, C, lambda o: b_copy(o).wait_recv())
-    if C <= 8:
-        for o in range(1, C):
-            piece = piece + wc[o]
+        to = lax.rem(index + o, peers)
+        rows = pl.ds(pl.multiple_of(to * piece_rows, 8), piece_rows)
+        r, c = at_peer(o)
+        return copy(whalf.at[rows, :], wr.at[o], b_send.at[o], b_recv.at[o], r, c)
+
+    loop(1, peers, lambda o: b_copy(o).start())
+    my_rows = pl.ds(pl.multiple_of(index * piece_rows, 8), piece_rows)
+    piece = whalf[my_rows, :]
+    loop(1, peers, lambda o: b_copy(o).wait_recv())
+    if peers <= 32:
+        for o in range(1, peers):
+            piece = piece + wr[o]
     else:
-        piece = lax.fori_loop(1, C, lambda o, acc: acc + wc[o], piece)
-    mine_rows = pl.ds(pl.multiple_of(me_c * cc, 8), cc)
-    wd[mine_rows, :] = piece
+        piece = lax.fori_loop(1, peers, lambda o, acc: acc + wr[o], piece)
+    obuf[core, my_rows, :] = piece
 
     def c_copy(o):
-        return copy(wd.at[mine_rows, :], wd.at[mine_rows, :], c_send.at[o], c_recv.at[o], me_r, at_col(o))
-
-    loop(1, C, lambda o: c_copy(o).start())
-    loop(1, C, lambda o: c_copy(o).wait_recv())
-    my_out = pl.ds(pl.multiple_of(me_r * cr, 8), cr)
-
-    def d_copy(o):
-        return copy(wd.at[pl.ds(0, cr), :], obuf.at[my_out, :], d_send.at[o], d_recv.at[o], at_row(o), me_c)
-
-    loop(1, R, lambda o: d_copy(o).start())
-    obuf[my_out, :] = wd[0:cr, :]
-    loop(1, R, lambda o: d_copy(o).wait_recv())
-    grad_out[...] = obuf[0:width, :]
+        r, c = at_peer(o)
+        ref = obuf.at[core, my_rows, :]
+        return copy(ref, ref, c_send.at[o], c_recv.at[o], r, c)
+
+    loop(1, peers, lambda o: c_copy(o).start())
+    loop(1, peers, lambda o: c_copy(o).wait_recv())
+    mine_done = obuf.at[core, pl.ds(0, half), :]
+    d_copy = copy(mine_done, mine_done, d_send, d_recv, me_r, sib)
+    d_copy.start()
+    my_half = pl.ds(pl.multiple_of(core * half, 8), half)
+    grad_out[my_half, :] = obuf[core, 0:half, :]
+    d_copy.wait_recv()
+    its_half = pl.ds(pl.multiple_of((1 - core) * half, 8), half)
+    grad_out[its_half, :] = obuf[1 - core, 0:half, :]
 
     for h in range(halves):
         loop(1, chips, lambda o: far(h, o).wait_send())
@@ -362,10 +369,19 @@
         loop(1, chips, lambda o: near(h, o).wait_send())
         loop(1, R, lambda o: part_copy(h, o).wait_send())
         loop(1, R, lambda o: agg_copy(h, o).wait_send())
-    loop(1, R, lambda o: a_copy(o).wait_send())
-    loop(1, C, lambda o: b_copy(o).wait_send())
-    loop(1, C, lambda o: c_copy(o).wait_send())
-    loop(1, R, lambda o: d_copy(o).wait_send())
+    a_copy.wait_send()
+    loop(1, peers, lambda o: b_copy(o).wait_send())
+    loop(1, peers, lambda o: c_copy(o).wait_send())
+    d_copy.wait_send()
+
+
+def hand_over(loss, grad, loss_out, grad_out, sems):
+    first = pltpu.make_async_copy(loss, loss_out, sems.at[0])
+    second = pltpu.make_async_copy(grad, grad_out, sems.at[1])
+    second.start()
+    first.start()
+    first.wait()
+    second.wait()
 
 
 def up(n, d, unit):
@@ -380,11 +396,10 @@
     C = lax.axis_size("col")
     group = R * nodes
     chips = C // 2
-    cr = up(width, R, 8)
-    cc = up(cr, C, 8)
+    peers = R * chips
+    piece_rows = up(width // 2, peers, 8)
     vmem = pl.BlockSpec(memory_space=pltpu.VMEM)
     held = pl.BlockSpec(memory_space=pl.ANY)
-    smem = pl.BlockSpec(memory_space=pltpu.SMEM)
     sem = pltpu.SemaphoreType.DMA
     loss, grad = pl.pallas_call(
         functools.partial(step_kernel, R, C),
@@ -392,11 +407,14 @@
             jax.ShapeDtypeStruct((nodes,), F32),
             jax.ShapeDtypeStruct((width, width), F32),
         ),
-        in_specs=[held, held, held, smem, smem, vmem, held],
+        in_specs=[held] * 7,
         out_specs=(vmem, vmem),
         scratch_shapes=[
             pltpu.VMEM(weight.shape, BF16),
             pltpu.VMEM(tiles.shape, BF16),
+            pltpu.SMEM(tile_pos.shape, jnp.int32),
+            pltpu.SMEM(edge_keep.shape, jnp.int32),
+            pltpu.VMEM(feature_keep.shape, jnp.int32),
             pltpu.VMEM(negatives.shape, jnp.int32),
             pltpu.VMEM((negatives.shape[1], negatives.shape[1]), BF16),
             pltpu.VMEM(negatives.shape, jnp.int32),
@@ -410,23 +428,33 @@
             pltpu.VMEM((R, 2, nodes, width), BF16),
             pltpu.VMEM((R, 2, nodes, 1), F32),
             pltpu.VMEM((R, 2, nodes, 128), F32),
-            pltpu.VMEM((width, 2 * width), F32),
-            pltpu.VMEM((R * cr, width), F32),
-            pltpu.VMEM((R, cr, width), F32),
-            pltpu.VMEM((C * cc, width), F32),
-            pltpu.VMEM((C, cc, width), F32),
-            pltpu.VMEM((C * cc, width), F32),
-            pltpu.VMEM((R * cr, width), F32),
+            pltpu.VMEM((R, width, 2 * nodes), BF16),
+            pltpu.VMEM((R, 2 * nodes, 2 * width), BF16),
+            pltpu.VMEM((width, width), F32),
+            pltpu.VMEM((width // 2, width), F32),
+            pltpu.VMEM((peers * piece_rows, width), F32),
+            pltpu.VMEM((peers, piece_rows, width), F32),
+            pltpu.VMEM((2, peers * piece_rows, width), F32),
             sem((halves, chips)), sem((halves, chips)), sem((halves, chips)), sem((halves, chips)),
             sem((halves, R)), sem((halves, R)), sem((halves, R)), sem((halves, R)),
-            sem((R,)), sem((R,)), sem((C,)), sem((C,)),
-            sem((C,)), sem((C,)), sem((R,)), sem((R,)), sem((3 + halves,)),
+            sem, sem, sem((peers,)), sem((peers,)),
+            sem((peers,)), sem((peers,)), sem, sem, sem((6 + halves,)),
         ],
         compiler_params=pltpu.CompilerParams(
             collective_id=0, has_side_effects=True, vmem_limit_bytes=60 << 20
         ),
     )(features, weight, tiles, tile_pos, edge_keep, feature_keep, negatives)
-    return loss, grad
+    return pl.pallas_call(
+        hand_over,
+        out_shape=(
+            jax.ShapeDtypeStruct((nodes,), F32),
+            jax.ShapeDtypeStruct((width, width), F32),
+        ),
+        in_specs=[held] * 2,
+        out_specs=(held, held),
+        scratch_shapes=[sem((2,))],
+        compiler_params=pltpu.CompilerParams(vmem_limit_bytes=60 << 20),
+    )(loss, grad)
 
 
 def solution(mesh):

time: 51.5 us -> 54.1 us (1.050)
  Pallas kernels: 47.9 us -> 53.3 us
  local copies, waits for them, and re-layouts: 2.74 us -> 0 us
    pallas_call x0 -> x1, Pallas kernels: none -> 9.08 us  [shards(): pl.pallas_call(hand_over, out_shape=(jax.ShapeDtypeStruct((nodes,), F32),...]
    pallas_call x1, Pallas kernels: 47.9 us -> 44.3 us  [shards(): pl.pallas_call(functools.partial(step_kernel, R, C), out_shape=(jax.Shape...]
    unnamed x4 -> x0, local copies, waits for them, and re-layouts: 2.74 us -> none
where the time goes in v4:
time: 54.1 us; the launch traced here: 54 us
  Pallas kernels  53.3 us (99%)
  between operations  0.64 us (1%)
    pallas_call x1, Pallas kernels, shards(): pl.pallas_call(functools.partial(step_kernel, R, C), out_shape=(jax.Shape...  44.3 us
    pallas_call x1, Pallas kernels, shards(): pl.pallas_call(hand_over, out_shape=(jax.ShapeDtypeStruct((nodes,), F32),...  9.08 us

profile of v4, /device:TPU:0, one launch (start us, length us, event | category | flops | bytes accessed | tf_op | source)
XLA Modules:
  0.0 54.0 jit_solution(14857934477963062818)
XLA Ops:
  0.6 44.3 %shard_map.86 = (f32[128]{0:T(128)}, f32[256,256]{1,0:T(8,128)}) custom-call(bf16[128,256]{1,0:T(8,128)(2,1)} %feat.1, bf16[256,256]{1,0:T(8,128)(2,1)} %weight_in.1, bf16[12,128,128]{2,1,0:T(8,128)(2,1)} %tiles_in.1, s32[12]{0:T(128)} %pos_in.1, s32[2,12]{1,0:T(2,128)} %keep_in.1, s32[2,256]{1,0:T(2,128)} %fkeep_in.1, s32[128,1024]{1,0:T(8,128)} %neg_in.1), custom_call_target="tpu_custom_call" | custom-call | tf_op jit(solution)/shard_map/pallas_call | solution.py:404
  44.9 9.1 %shard_map.87 = (f32[128]{0:T(128)}, f32[256,256]{1,0:T(8,128)}) custom-call(f32[128]{0:T(128)} %get-tuple-element.4.loss, f32[256,256]{1,0:T(8,128)} %get-tuple-element.5.grad), custom_call_target="tpu_custom_call" | custom-call | tf_op jit(solution)/shard_map/pallas_call | solution.py:447

commit v5 on v4

--- a/solution.py
+++ b/solution.py
@@ -136,6 +136,7 @@
     barrier = pltpu.get_barrier_semaphore()
     loop(1, peers, lambda o: pl.semaphore_signal(barrier, inc=1, device_id=at_peer(o), device_id_type=MESH))
     pl.semaphore_signal(barrier, inc=1, device_id=(me_r, sib), device_id_type=MESH)
+    spread_matrix(matrix)
     pl.semaphore_wait(barrier, peers)
 
     def far(h, o):
@@ -151,7 +152,6 @@
     for h in range(halves):
         loop(1, chips, lambda o: far(h, o).start())
         near(h, 0).start()
-    spread_matrix(matrix)
     loads[0].wait()
     spread(neg, matrix, spread_ref)
     tall = 32
@@ -174,7 +174,7 @@
         for v in range(2):
             total = None
             for k in range(slots):
-                term = prod[k] * jnp.where(here[k], live[v][k], 0).astype(F32)
+                term = prod[h, k] * jnp.where(here[k], live[v][k], 0).astype(F32)
                 total = term if total is None else total + term
             pbuf[h, o, v] = total.astype(BF16)
 
@@ -190,20 +190,20 @@
         if h == 0:
             loads[1].wait()
         for k in range(slots):
-            prod[k] = jnp.dot(tiles[k], xg[h][lax.rem(where[k], C)], preferred_element_type=F32)
+            prod[h, k] = jnp.dot(tiles[k], xg[h][lax.rem(where[k], C)], preferred_element_type=F32)
 
         def part_send(o):
             part(h, o)
             part_copy(h, o).start()
 
         loop(1, R, part_send)
-        part(h, 0)
 
     def agg_copy(h, o):
         ref = gbuf.at[me_r, :, :, h * 128 : (h + 1) * 128]
         return copy(ref, ref, g_send.at[h, o], g_recv.at[h, o], at_row(o), me_c)
 
     for h in range(halves):
+        part(h, 0)
         loop(1, R, lambda o: part_copy(h, o).wait_recv())
         for v in range(2):
             total = pbuf[h, 0, v].astype(F32)
@@ -270,7 +270,6 @@
     tot1 = epos + row_sum(0)
     tot2 = epos + row_sum(1)
     loss = 0.5 * (jnp.log(tot1) - pos + (jnp.log(tot2) - pos))
-    loss_out[...] = jnp.broadcast_to(loss, (nodes, 128)).T[0]
     both = epos / tot1 + epos / tot2 - 2.0
     coef = 1.0 / (2.0 * tau * float(R * C * nodes) ** 0.5)
 
@@ -308,23 +307,26 @@
         me_r, coef * (both * h2f + acc1 + own1), coef * (both * h1f + acc2 + own2)
     )
 
-    def grad_term(r):
-        return jnp.dot(turned[r], dzb[r], preferred_element_type=F32)
-
-    if R <= 8:
-        terms = grad_term(0)
-        for r in range(1, R):
-            terms = terms + grad_term(r)
-    else:
-        terms = lax.fori_loop(1, R, lambda r, acc: acc + grad_term(r), grad_term(0))
-    wbuf[...] = terms[:, :width] + terms[:, width:]
-
     half = width // 2
-    a_copy = copy(
-        wbuf.at[pl.ds(pl.multiple_of((1 - core) * half, 8), half), :], wsib, a_send, a_recv, me_r, sib
-    )
+
+    def grad_half(side):
+        rows = pl.ds(pl.multiple_of(side * half, 16), half)
+
+        def term(r):
+            return jnp.dot(turned[r, rows, :], dzb[r], preferred_element_type=F32)
+
+        if R <= 8:
+            terms = term(0)
+            for r in range(1, R):
+                terms = terms + term(r)
+        else:
+            terms = lax.fori_loop(1, R, lambda r, acc: acc + term(r), term(0))
+        return terms[:, :width] + terms[:, width:]
+
+    wbuf[...] = grad_half(1 - core)
+    a_copy = copy(wbuf, wsib, a_send, a_recv, me_r, sib)
     a_copy.start()
-    own = wbuf[pl.ds(pl.multiple_of(core * half, 8), half), :]
+    own = grad_half(core)
     if whalf.shape[0] > half:
         whalf[...] = jnp.zeros_like(whalf)
     a_copy.wait_recv()
@@ -337,6 +339,7 @@
         return copy(whalf.at[rows, :], wr.at[o], b_send.at[o], b_recv.at[o], r, c)
 
     loop(1, peers, lambda o: b_copy(o).start())
+    loss_out[...] = jnp.broadcast_to(loss, (nodes, 128)).T[0]
     my_rows = pl.ds(pl.multiple_of(index * piece_rows, 8), piece_rows)
     piece = whalf[my_rows, :]
     loop(1, peers, lambda o: b_copy(o).wait_recv())
@@ -375,13 +378,22 @@
     d_copy.wait_send()
 
 
-def hand_over(loss, grad, loss_out, grad_out, sems):
-    first = pltpu.make_async_copy(loss, loss_out, sems.at[0])
-    second = pltpu.make_async_copy(grad, grad_out, sems.at[1])
-    second.start()
-    first.start()
-    first.wait()
-    second.wait()
+def hand_over(loss, grad, loss_out, grad_out, loss_buf, grad_buf, in_sems, out_sems):
+    chunks = out_sems.shape[0] - 1
+    rows = grad.shape[0] // chunks
+    ins = [pltpu.make_async_copy(loss, loss_buf, in_sems.at[chunks])]
+    outs = [pltpu.make_async_copy(loss_buf, loss_out, out_sems.at[chunks])]
+    for i in range(chunks):
+        part = pl.ds(i * rows, rows)
+        ins.append(pltpu.make_async_copy(grad.at[part, :], grad_buf.at[part, :], in_sems.at[i]))
+        outs.append(pltpu.make_async_copy(grad_buf.at[part, :], grad_out.at[part, :], out_sems.at[i]))
+    for move in ins:
+        move.start()
+    for move, then in zip(ins, outs):
+        move.wait()
+        then.start()
+    for move in outs:
+        move.wait()
 
 
 def up(n, d, unit):
@@ -420,7 +432,7 @@
             pltpu.VMEM(negatives.shape, jnp.int32),
             pltpu.VMEM((nodes, group), F32),
             [pltpu.VMEM((C, nodes, 128), BF16)] * halves,
-            pltpu.VMEM((slots, 128, 128), F32),
+            pltpu.VMEM((halves, slots, 128, 128), F32),
             pltpu.VMEM((halves, R, 2, nodes, 128), BF16),
             pltpu.VMEM((halves, R, 2, nodes, 128), BF16),
             pltpu.VMEM((R, 2, nodes, width), BF16),
@@ -430,7 +442,7 @@
             pltpu.VMEM((R, 2, nodes, 128), F32),
             pltpu.VMEM((R, width, 2 * nodes), BF16),
             pltpu.VMEM((R, 2 * nodes, 2 * width), BF16),
-            pltpu.VMEM((width, width), F32),
+            pltpu.VMEM((width // 2, width), F32),
             pltpu.VMEM((width // 2, width), F32),
             pltpu.VMEM((peers * piece_rows, width), F32),
             pltpu.VMEM((peers, piece_rows, width), F32),
@@ -452,7 +464,7 @@
         ),
         in_specs=[held] * 2,
         out_specs=(held, held),
-        scratch_shapes=[sem((2,))],
+        scratch_shapes=[pltpu.VMEM((nodes,), F32), pltpu.VMEM((width, width), F32), sem((5,)), sem((5,))],
         compiler_params=pltpu.CompilerParams(vmem_limit_bytes=60 << 20),
     )(loss, grad)
 

time: 54.1 us -> 46.6 us (0.86)
  Pallas kernels: 53.3 us -> 45.8 us
    pallas_call x1, Pallas kernels: 9.08 us -> 1.65 us  [shards(): pl.pallas_call(hand_over, out_shape=(jax.ShapeDtypeStruct((nodes,), F32),...]
where the time goes in v5:
time: 46.6 us; the launch traced here: 46.4 us
  Pallas kernels  45.8 us (98%)
  between operations  0.64 us (1%)
    pallas_call x1, Pallas kernels, shards(): pl.pallas_call(functools.partial(step_kernel, R, C), out_shape=(jax.Shape...  44.1 us
    pallas_call x1, Pallas kernels, shards(): pl.pallas_call(hand_over, out_shape=(jax.ShapeDtypeStruct((nodes,), F32),...  1.65 us

profile of v5, /device:TPU:0, one launch (start us, length us, event | category | flops | bytes accessed | tf_op | source)
XLA Modules:
  0.0 46.4 jit_solution(9252237498647731313)
XLA Ops:
  0.6 44.1 %shard_map.86 = (f32[128]{0:T(128)}, f32[256,256]{1,0:T(8,128)}) custom-call(bf16[128,256]{1,0:T(8,128)(2,1)} %feat.1, bf16[256,256]{1,0:T(8,128)(2,1)} %weight_in.1, bf16[12,128,128]{2,1,0:T(8,128)(2,1)} %tiles_in.1, s32[12]{0:T(128)} %pos_in.1, s32[2,12]{1,0:T(2,128)} %keep_in.1, s32[2,256]{1,0:T(2,128)} %fkeep_in.1, s32[128,1024]{1,0:T(8,128)} %neg_in.1), custom_call_target="tpu_custom_call" | custom-call | tf_op jit(solution)/shard_map/pallas_call | solution.py:416
  44.8 1.7 %shard_map.87 = (f32[128]{0:T(128)}, f32[256,256]{1,0:T(8,128)}) custom-call(f32[128]{0:T(128)} %get-tuple-element.4.loss, f32[256,256]{1,0:T(8,128)} %get-tuple-element.5.grad), custom_call_target="tpu_custom_call" | custom-call | tf_op jit(solution)/shard_map/pallas_call | solution.py:459

commit v6 on v5

--- a/solution.py
+++ b/solution.py
@@ -102,11 +102,20 @@
     core = me_c % 2
     sib = chip * 2 + (1 - core)
 
+    paired = R <= 8 and R & (R - 1) == 0
+
+    def partner(o):
+        to = me_r
+        for bit in range(3):
+            if o >> bit & 1:
+                to = to + (1 - 2 * (me_r // 2**bit % 2)) * 2**bit
+        return to
+
     def at_row(o):
-        return lax.rem(me_r + o, R)
+        return partner(o) if paired else lax.rem(me_r + o, R)
 
     def from_row(o):
-        return lax.rem(me_r + R - o, R)
+        return partner(o) if paired else lax.rem(me_r + R - o, R)
 
     index = me_r * chips + chip
 
@@ -156,8 +165,7 @@
     spread(neg, matrix, spread_ref)
     tall = 32
     turns = nodes // tall
-    for i in range(turns // 2):
-        count_rows(i, tall, spread_ref, cnt)
+    count_rows(0, tall, spread_ref, cnt)
 
     for load in loads[3 + halves :]:
         load.wait()
@@ -196,7 +204,9 @@
             part(h, o)
             part_copy(h, o).start()
 
-        loop(1, R, part_send)
+        loop(1, R, lambda o: part_send(R - o))
+
+    count_rows(1, tall, spread_ref, cnt)
 
     def agg_copy(h, o):
         ref = gbuf.at[me_r, :, :, h * 128 : (h + 1) * 128]
@@ -215,7 +225,7 @@
             total = total * fkeep[v : v + 1, h * 128 : (h + 1) * 128].astype(F32)
             gbuf[me_r, v, :, h * 128 : (h + 1) * 128] = total.astype(BF16)
         loop(1, R, lambda o: agg_copy(h, o).start())
-    for i in range(turns // 2, turns):
+    for i in range(2, turns):
         count_rows(i, tall, spread_ref, cnt)
     loads[2].wait()
 

time: 46.6 us -> 46.2 us (level)
  Pallas kernels: 45.8 us -> 45.3 us
where the time goes in v6:
time: 46.2 us; the launch traced here: 46 us
  Pallas kernels  45.3 us (98%)
  between operations  0.64 us (1%)
    pallas_call x1, Pallas kernels, shards(): pl.pallas_call(functools.partial(step_kernel, R, C), out_shape=(jax.Shape...  43.7 us
    pallas_call x1, Pallas kernels, shards(): pl.pallas_call(hand_over, out_shape=(jax.ShapeDtypeStruct((nodes,), F32),...  1.65 us

profile of v6, /device:TPU:0, one launch (start us, length us, event | category | flops | bytes accessed | tf_op | source)
XLA Modules:
  0.0 46.0 jit_solution(7919098197854024960)
XLA Ops:
  0.6 43.7 %shard_map.86 = (f32[128]{0:T(128)}, f32[256,256]{1,0:T(8,128)}) custom-call(bf16[128,256]{1,0:T(8,128)(2,1)} %feat.1, bf16[256,256]{1,0:T(8,128)(2,1)} %weight_in.1, bf16[12,128,128]{2,1,0:T(8,128)(2,1)} %tiles_in.1, s32[12]{0:T(128)} %pos_in.1, s32[2,12]{1,0:T(2,128)} %keep_in.1, s32[2,256]{1,0:T(2,128)} %fkeep_in.1, s32[128,1024]{1,0:T(8,128)} %neg_in.1), custom_call_target="tpu_custom_call" | custom-call | tf_op jit(solution)/shard_map/pallas_call | solution.py:426
  44.3 1.7 %shard_map.87 = (f32[128]{0:T(128)}, f32[256,256]{1,0:T(8,128)}) custom-call(f32[128]{0:T(128)} %get-tuple-element.4.loss, f32[256,256]{1,0:T(8,128)} %get-tuple-element.5.grad), custom_call_target="tpu_custom_call" | custom-call | tf_op jit(solution)/shard_map/pallas_call | solution.py:469

commit v7 on v6

--- a/solution.py
+++ b/solution.py
@@ -165,7 +165,6 @@
     spread(neg, matrix, spread_ref)
     tall = 32
     turns = nodes // tall
-    count_rows(0, tall, spread_ref, cnt)
 
     for load in loads[3 + halves :]:
         load.wait()
@@ -192,6 +191,8 @@
             near(h, o).start()
 
         loop(1, chips, pass_on)
+        if h == 0:
+            count_rows(0, tall, spread_ref, cnt)
         near(h, 0).wait_recv()
         loop(1, chips, lambda o: near(h, o).wait_recv())
         loads[3 + h].wait()

time: 46.2 us -> 47.3 us (1.024)
  Pallas kernels: 45.3 us -> 46.5 us
    pallas_call x1, Pallas kernels: 43.7 us -> 44.8 us  [shards(): pl.pallas_call(functools.partial(step_kernel, R, C), out_shape=(jax.Shape...]
where the time goes in v7:
time: 47.3 us; the launch traced here: 47.1 us
  Pallas kernels  46.5 us (98%)
  between operations  0.64 us (1%)
    pallas_call x1, Pallas kernels, shards(): pl.pallas_call(functools.partial(step_kernel, R, C), out_shape=(jax.Shape...  44.8 us
    pallas_call x1, Pallas kernels, shards(): pl.pallas_call(hand_over, out_shape=(jax.ShapeDtypeStruct((nodes,), F32),...  1.65 us

profile of v7, /device:TPU:0, one launch (start us, length us, event | category | flops | bytes accessed | tf_op | source)
XLA Modules:
  0.0 47.1 jit_solution(2814437348519916041)
XLA Ops:
  0.6 44.8 %shard_map.86 = (f32[128]{0:T(128)}, f32[256,256]{1,0:T(8,128)}) custom-call(bf16[128,256]{1,0:T(8,128)(2,1)} %feat.1, bf16[256,256]{1,0:T(8,128)(2,1)} %weight_in.1, bf16[12,128,128]{2,1,0:T(8,128)(2,1)} %tiles_in.1, s32[12]{0:T(128)} %pos_in.1, s32[2,12]{1,0:T(2,128)} %keep_in.1, s32[2,256]{1,0:T(2,128)} %fkeep_in.1, s32[128,1024]{1,0:T(8,128)} %neg_in.1), custom_call_target="tpu_custom_call" | custom-call | tf_op jit(solution)/shard_map/pallas_call | solution.py:427
  45.5 1.7 %shard_map.87 = (f32[128]{0:T(128)}, f32[256,256]{1,0:T(8,128)}) custom-call(f32[128]{0:T(128)} %get-tuple-element.4.loss, f32[256,256]{1,0:T(8,128)} %get-tuple-element.5.grad), custom_call_target="tpu_custom_call" | custom-call | tf_op jit(solution)/shard_map/pallas_call | solution.py:470
